TPU v7x, 128 devices: a whole 4x4x4 slice. The times are simulated.
128 devices in a mesh: wide: 32 (over x, y_lo, z), narrow: 4 (over y_hi, core).
Axes of the slice: x: 4, y: 4 (y_hi: 2, y_lo: 2; y = y_hi * 2 + y_lo), z: 4, core: 2. Of those that a mesh axis runs over, the one named last changes fastest.
Arguments:
- hidden: bfloat16 [2048, 4096], P('narrow', 'wide'), may hold values from -6 to 6
- attn_gain: float32 [4096], replicated, may hold values from 0.5 to 1.5
- query_weight: bfloat16 [4096, 4096], P(None, 'wide'), may hold values from -0.09375 to 0.09375
- key_weight: bfloat16 [4096, 1024], P('wide'), may hold values from -0.1875 to 0.1875
- value_weight: bfloat16 [4096, 1024], P('wide'), may hold values from -0.1875 to 0.1875
- out_weight: bfloat16 [4096, 4096], P('wide'), may hold values from -0.09375 to 0.09375
- cache_key: bfloat16 [8, 512, 128], replicated, may hold values from -600 to 600
- cache_value: bfloat16 [8, 512, 128], replicated, may hold values from -6 to 6
- mlp_gain: float32 [4096], replicated, may hold values from 0.5 to 1.5
- router_weight: bfloat16 [4096, 16], replicated, may hold values from -0.09375 to 0.09375
- expert_ids: int32 [2048, 2], P('narrow'), may hold values from 0 to 15, all different within a row; in each aligned block of 16 rows (0 to 15, 16 to 31, ...) at most 4 rows name the same one
- gate_weight: bfloat16 [32, 4096, 3200], P('wide', None, 'narrow'), may hold values from -0.09375 to 0.09375
- up_weight: bfloat16 [32, 4096, 3200], P('wide', None, 'narrow'), may hold values from -0.09375 to 0.09375
- down_weight: bfloat16 [32, 3200, 4096], P('wide', 'narrow'), may hold values from -0.078125 to 0.078125
Outputs:
- layer_out: bfloat16 [2048, 4096], P('narrow', 'wide')
Inputs may be any that keep to these rules, and one draw needn't show every extreme that they name: `expert_ids`: in each aligned block of 16 rows no expert is named by more than 4 rows, and in every block some expert by exactly 4; the two experts of a row differ.
All inputs are finite; a program needn't handle non-finite values.
Results may differ from a plain program's by a relative error of at most 0.012.
The roundings to bfloat16 on the way count: a program that leaves them out, or rounds other values in their place, can miss the bound.
Values may be sent and summed in bfloat16 or wider, within the bound.
A program may use at most 128 MiB of HBM per device.

v0:
```python
import jax
import jax.numpy as jnp
from jax import lax
from jax.sharding import PartitionSpec as P

SPLIT = 2
CAPD = 4


epsilon = 1e-05


def layer_normed(values, gain):
    average = jnp.mean(values, axis=-1, keepdims=True)
    centered = values - average
    variance = jnp.mean(centered * centered, axis=-1, keepdims=True)
    return centered * lax.rsqrt(variance + epsilon) * gain


def slot_targets(routing, experts, capacity):
    blocks = routing.shape[0]
    flat_ids = routing.reshape(blocks, -1)
    onehot = (flat_ids[:, :, None] == jnp.arange(experts, dtype=jnp.int32)[None, None, :]).astype(
        jnp.int32
    )
    earlier = jnp.cumsum(onehot, axis=1) - onehot
    position = jnp.sum(earlier * onehot, axis=2)
    return (flat_ids * capacity + position).reshape(routing.shape)


def fill_buffer(normed, target, slot_count):
    matches = (target[:, :, :, None] == jnp.arange(slot_count, dtype=jnp.int32)).astype(
        jnp.bfloat16
    )
    placing = jnp.sum(matches, axis=2)
    return jnp.einsum("btj,btd->bjd", placing, normed, preferred_element_type=jnp.float32).astype(
        jnp.bfloat16
    )


def pair_weights(logits, routing):
    picked = jnp.take_along_axis(logits, routing, axis=-1)
    leading = jax.nn.sigmoid(picked[..., 0] - picked[..., 1])
    return jnp.stack([leading, 1.0 - leading], axis=-1)


def gather_back(results, target, weights):
    blocks, slot_count = (results.shape[0], results.shape[1])
    flat_rows = results.reshape(blocks * slot_count, results.shape[2])
    row_index = target + (jnp.arange(blocks, dtype=jnp.int32) * slot_count)[:, None, None]
    picked = jnp.take(flat_rows, row_index.reshape(-1), axis=0).reshape(
        target.shape + (results.shape[2],)
    )
    return jnp.sum(picked * weights[..., None], axis=2)


def expert_terms(arrived, w_gate, w_up, w_down):
    gate_term = jnp.einsum("gscd,sdf->gscf", arrived, w_gate, preferred_element_type=jnp.float32)
    up_term = jnp.einsum("gscd,sdf->gscf", arrived, w_up, preferred_element_type=jnp.float32)
    active = (jax.nn.silu(gate_term) * up_term).astype(jnp.bfloat16)
    return jnp.einsum("gscf,sfd->gscd", active, w_down, preferred_element_type=jnp.float32)


def attend(queries, all_keys, all_values, first_row, context):
    row_count, heads_here, head_size = queries.shape
    kv_here = all_keys.shape[0]
    grouped = queries.reshape(row_count, kv_here, heads_here // kv_here, head_size)
    scale_factor = head_size ** (-0.5)
    scores = (
        jnp.einsum("rgqd,gkd->gqrk", grouped, all_keys, preferred_element_type=jnp.float32)
        * scale_factor
    )
    row_ids = first_row + jnp.arange(row_count, dtype=jnp.int32)
    key_ids = jnp.arange(all_keys.shape[1], dtype=jnp.int32) - context
    allowed = key_ids[None, :] <= row_ids[:, None]
    scores = jnp.where(allowed[None, None], scores, -1e30)
    highest = jnp.max(scores, axis=3, keepdims=True)
    weights = jnp.exp(scores - highest)
    weights = (weights / jnp.sum(weights, axis=3, keepdims=True)).astype(jnp.bfloat16)
    mixed = jnp.einsum(
        "gqrk,gkd->rgqd", weights, all_values, preferred_element_type=jnp.float32
    ).astype(jnp.bfloat16)
    return mixed.reshape(row_count, heads_here, head_size)


def body(
    hidden,
    attn_gain,
    query_weight,
    key_weight,
    value_weight,
    out_weight,
    cache_key,
    cache_value,
    mlp_gain,
    router_weight,
    expert_ids,
    gate_weight,
    up_weight,
    down_weight,
):
    wide_count = lax.axis_size("wide")
    wide_index = lax.axis_index("wide")
    narrow_index = lax.axis_index("narrow")
    full_rows = lax.all_gather(hidden, "wide", axis=1, tiled=True)
    row_count, feature_count = full_rows.shape
    kv_total, context, head_size = cache_key.shape
    heads_here = query_weight.shape[1] // head_size
    share = heads_here * wide_count // kv_total
    kv_here = max(heads_here // share, 1)
    kv_start = wide_index * heads_here // share
    normed = layer_normed(full_rows.astype(jnp.float32), attn_gain).astype(jnp.bfloat16)
    queries = jnp.dot(normed, query_weight, preferred_element_type=jnp.float32).astype(jnp.bfloat16)
    feature_share = key_weight.shape[0]
    normed_part = lax.dynamic_slice_in_dim(normed, wide_index * feature_share, feature_share, 1)
    key_term = jnp.dot(normed_part, key_weight, preferred_element_type=jnp.float32)
    value_term = jnp.dot(normed_part, value_weight, preferred_element_type=jnp.float32)
    key_cols, value_cols = lax.psum((key_term, value_term), "wide")
    key_cols = key_cols.astype(jnp.bfloat16)
    value_cols = value_cols.astype(jnp.bfloat16)
    fresh_keys = lax.dynamic_slice_in_dim(key_cols, kv_start * head_size, kv_here * head_size, 1)
    fresh_values = lax.dynamic_slice_in_dim(
        value_cols, kv_start * head_size, kv_here * head_size, 1
    )
    span_key_rows, span_value_rows = (
        lax.all_gather(fresh_keys, "narrow", axis=0, tiled=True),
        lax.all_gather(fresh_values, "narrow", axis=0, tiled=True),
    )
    own_cache_key = lax.dynamic_slice_in_dim(cache_key, kv_start, kv_here, 0)
    own_cache_value = lax.dynamic_slice_in_dim(cache_value, kv_start, kv_here, 0)
    all_keys = jnp.concatenate(
        [own_cache_key, span_key_rows.reshape(-1, kv_here, head_size).transpose(1, 0, 2)], axis=1
    )
    all_values = jnp.concatenate(
        [own_cache_value, span_value_rows.reshape(-1, kv_here, head_size).transpose(1, 0, 2)],
        axis=1,
    )
    attended = attend(
        queries.reshape(row_count, heads_here, head_size),
        all_keys,
        all_values,
        narrow_index * row_count,
        context,
    )
    attended = attended.reshape(row_count, heads_here * head_size)
    experts = router_weight.shape[1]
    capacity = CAPD
    slot_count = experts * SPLIT
    slots_here = gate_weight.shape[0]
    block_rows = row_count // wide_count
    head_mix = lax.psum_scatter(
        jnp.dot(attended, out_weight, preferred_element_type=jnp.float32),
        "wide",
        scatter_dimension=0,
        tiled=True,
    )
    own_rows = lax.dynamic_slice_in_dim(full_rows, wide_index * block_rows, block_rows, 0)
    residual = (own_rows.astype(jnp.float32) + head_mix).astype(jnp.bfloat16)
    normed_two = layer_normed(residual.astype(jnp.float32), mlp_gain).astype(jnp.bfloat16)
    logits = jnp.dot(normed_two, router_weight, preferred_element_type=jnp.float32)[None]
    routing = lax.dynamic_slice_in_dim(expert_ids, wide_index * block_rows, block_rows, 0)[None]
    target = slot_targets(routing, experts, capacity)
    buffer = fill_buffer(normed_two[None], target, experts * capacity)
    buffer = jnp.broadcast_to(
        buffer.reshape(experts, 1, capacity, feature_count),
        (experts, SPLIT, capacity, feature_count),
    )
    arrived = lax.all_to_all(
        buffer.reshape(slot_count, capacity, feature_count),
        "wide",
        split_axis=0,
        concat_axis=0,
        tiled=True,
    )
    arrived = arrived.reshape(wide_count, slots_here, capacity, feature_count)
    partial_out = expert_terms(
        lax.all_gather(arrived, "narrow", axis=0, tiled=True), gate_weight, up_weight, down_weight
    )
    reduced = lax.psum_scatter(partial_out, "narrow", scatter_dimension=0, tiled=True).astype(
        jnp.bfloat16
    )
    returned = lax.all_to_all(reduced, "wide", split_axis=0, concat_axis=1, tiled=True)
    summed = jnp.sum(
        returned.reshape(1, experts, SPLIT, capacity, feature_count).astype(jnp.float32), axis=2
    )
    mixture = gather_back(
        summed.reshape(1, experts * capacity, feature_count), target, pair_weights(logits, routing)
    )
    result = (residual.astype(jnp.float32) + mixture[0]).astype(jnp.bfloat16)
    final_out = lax.all_to_all(result, "wide", split_axis=1, concat_axis=0, tiled=True)
    return final_out


def solution(mesh):
    placed = (
        P("narrow", "wide"),
        P(),
        P(None, "wide"),
        P("wide", None),
        P("wide", None),
        P("wide", None),
        P(),
        P(),
        P(),
        P(),
        P("narrow", None),
        P("wide", None, "narrow"),
        P("wide", None, "narrow"),
        P("wide", "narrow", None),
    )
    return jax.shard_map(
        body, mesh=mesh, in_specs=placed, out_specs=P("narrow", "wide"), check_vma=False
    )
```

profile of v0, /device:TPU:1, one launch (start us, length us, event | category | flops | bytes accessed | tf_op | source)
XLA Modules:
  0.0 778.9 jit_solution(16558529448970607368)
XLA Ops:
  6.5 0.7 all-gather.4.cloned.1.call-update
  7.4 0.9 constant_dynamic-slice_fusion.1
  8.3 0.9 constant_dynamic-slice_fusion.2
  9.2 122.6 %all-gather.4.cloned.1.call-done = bf16[512,4096]{1,0:T(8,128)(2,1)} async-done(((bf16[512,128]{1,0:T(8,128)(2,1)}), bf16[512,4096]{1,0:T(8,128)(2,1)}) %all-gather.4.cloned.1.call-update) | async-done | bytes 4194320 | tf_op jit(solution)/shard_map/all_gather | solution.py:105
  131.8 3.0 convert_reduce_fusion
  134.8 0.5 copy-done.2
  135.2 1.2 fusion.2
  136.5 2.3 fusion.4
  138.8 0.4 fusion.48
  139.3 1.5 copy-done.3
  140.7 1.8 fusion.50
  142.5 164.6 %all-reduce.2 = (bf16[512,1024]{1,0:T(8,128)(2,1)}, bf16[512,1024]{1,0:T(8,128)(2,1)}) all-reduce(f32[512,1024]{1,0:T(8,128)S(1)} %fusion.48, f32[512,1024]{1,0:T(8,128)} %fusion.50), channel_id=1, replica_groups=mesh['wide'=32,'narrow'=4] {'wide'}, use_global_device_ids=true, to_apply=%region_3.4 | all-reduce | flops 1048576 | bytes 6291456 | tf_op jit(solution)/shard_map/psum | solution.py:118
  307.1 0.9 dynamic-slice_convert_fusion
  308.0 51.3 %all_gather.14 = bf16[2048,128]{1,0:T(8,128)(2,1)S(1)} all-gather(bf16[512,128]{1,0:T(8,128)(2,1)S(1)} %dynamic-slice_convert_fusion), channel_id=1, replica_groups=mesh['wide'=32,'narrow'=4] {'narrow'}, dimensions={0}, use_global_device_ids=true | all-gather | bytes 655360 | tf_op jit(solution)/shard_map/all_gather | solution.py:126
  359.3 0.9 dynamic-slice_convert_fusion.1
  360.2 8.8 %all_gather.13 = bf16[2048,128]{1,0:T(8,128)(2,1)S(1)} all-gather(bf16[512,128]{1,0:T(8,128)(2,1)S(1)} %dynamic-slice_convert_fusion.1), channel_id=1, replica_groups=mesh['wide'=32,'narrow'=4] {'narrow'}, dimensions={0}, use_global_device_ids=true | all-gather | bytes 655360 | tf_op jit(solution)/shard_map/all_gather | solution.py:127
  369.0 8.2 %fusion.67 = (f32[512]{0:T(512)S(1)}, f32[1,1,512,2560]{2,3,1,0:T(8,128)}) fusion(bf16[512,4096]{1,0:T(8,128)(2,1)} %copy-done.3, bf16[4096,128]{1,0:T(8,128)(2,1)} %param.16, bf16[1,2048,128]{2,1,0:T(8,128)(2,1)S(1)} %bitcast.146, bf16[1,512,128]{2,1,0:T(8,128)(2,1)S(1)} %constant_dynamic-slice_fusion.1, s32[512]{0:T(512)S(1)} %iota_add_fusion.1, ...), kind=kOutput, calls=%fused_computation.96 | convolution fusion | flops 879033856 | bytes 11155456 | tf_op jit(solution)/shard_map/rgqd,gkd->gqrk/dot_general | solution.py:70
  377.2 3.2 fusion.14
  380.5 8.1 %fusion.33 = f32[512,4096]{1,0:T(8,128)} fusion(bf16[128,4096]{1,0:T(8,128)(2,1)S(1)} %copy-done, f32[512]{0:T(512)S(1)} %fusion.14, f32[1,1,512,2560]{2,3,1,0:T(8,128)} %get-tuple-element.16, f32[512]{0:T(512)S(1)} %get-tuple-element.15, bf16[1,2048,128]{2,1,0:T(8,128)(2,1)S(1)} %bitcast.147, bf16[1,512,128]{2,1,0:T(8,128)(2,1)S(1)} %constant_dynamic-slice_fusion.2), kind=kOutput, calls=%fused_computation.35 | convolution fusion | flops 877723648 | bytes 15339520 | tf_op jit(solution)/shard_map/dot_general | solution.py:152
  388.6 0.2 all-gather.6.cloned.1.call-start
  388.8 0.8 bitcast_or_fusion
  389.8 0.2 select_reduce_fusion
  390.3 149.6 %reduce-scatter.3.cloned.1.call-done = f32[16,4096]{1,0:T(8,128)} async-done(((f32[512,4096]{1,0:T(8,128)}), f32[16,4096]{1,0:T(8,128)}) %reduce-scatter.3.cloned.1.call-update) | async-done | bytes 262160 | tf_op jit(solution)/shard_map/reduce_scatter | solution.py:151
  539.9 1.1 convert_reduce_fusion.2
  541.0 0.2 fusion.43
  541.2 0.3 convolution_convert_fusion
  541.6 0.2 broadcast_in_dim.25
  541.8 0.5 broadcast_in_dim.26
  542.3 15.2 %all_to_all.33 = bf16[32,4,4096]{2,1,0:T(4,128)(2,1)S(1)} all-to-all(bf16[32,4,4096]{2,1,0:T(4,128)(2,1)S(1)} %bitcast.145), channel_id=1, replica_groups=mesh['wide'=32,'narrow'=4] {'wide'}, dimensions={0} | all-to-all | bytes 2097152 | tf_op jit(solution)/shard_map/all_to_all | solution.py:168
  557.4 1.6 copy.53
  559.1 63.2 %all-gather.6.cloned.1.call-done = bf16[128,4,4096]{2,0,1:T(8,128)(2,1)} async-done(((bf16[32,4,4096]{2,0,1:T(8,128)(2,1)}), bf16[128,4,4096]{2,0,1:T(8,128)(2,1)}) %all-gather.6.cloned.1.call-update) | async-done | bytes 4194320 | tf_op jit(solution)/shard_map/all_gather | solution.py:177
  622.3 7.6 fusion.9
  629.9 22.6 %fusion.11 = f32[128,1,4,4096]{3,0,2,1:T(8,128)} fusion(bf16[1,800,4096]{2,1,0:T(8,128)(2,1)} %param.27, bf16[128,4,4096]{2,0,1:T(8,128)(2,1)} %all-gather.6.cloned.1.call-done, bf16[1,4096,800]{1,2,0:T(8,128)(2,1)} %param.26, f32[128,4,800]{0,2,1:T(8,128)} %fusion.9), kind=kOutput, calls=%fused_computation.15 | convolution fusion | flops 6713344000 | bytes 27328512 | tf_op jit(solution)/shard_map/gscf,sfd->gscd/dot_general | solution.py:61
  652.7 77.6 %reduce-scatter.5.cloned.1.call-done = f32[32,1,4,4096]{3,0,2,1:T(8,128)} async-done(((f32[128,1,4,4096]{3,0,2,1:T(8,128)}), f32[32,1,4,4096]{3,0,2,1:T(8,128)}) %reduce-scatter.5.cloned.1.call-update) | async-done | bytes 2097168 | tf_op jit(solution)/shard_map/reduce_scatter | solution.py:179
  730.2 1.7 convert_element_type.116
  732.0 1.8 copy.54
  733.8 7.2 all-to-all-start.1
  741.2 0.1 copy.52
  741.3 0.2 fusion.63
  741.5 0.7 gather_fusion.1
  742.6 12.9 %all-to-all-done.1 = bf16[32,1,4,4096]{3,2,1,0:T(4,128)(2,1)S(1)} async-done(((bf16[32,1,4,4096]{3,2,1,0:T(4,128)(2,1)}), bf16[32,1,4,4096]{3,2,1,0:T(4,128)(2,1)S(1)}, u32[]{:S(2)}, u32[]{:S(2)}) %all-to-all-start.1) | async-done | bytes 1048608 | tf_op jit(solution)/shard_map/all_to_all | solution.py:182
  755.5 0.6 convert_reduce_fusion.1
  756.1 0.4 reshape_reshape.9
  756.5 0.7 gather_fusion
  757.2 0.3 gather.13
  757.6 0.8 multiply_reduce_fusion
  758.4 13.3 %all_to_all.34 = bf16[16,32,128]{2,0,1:T(8,128)(2,1)S(1)} all-to-all(bf16[16,32,128]{2,0,1:T(8,128)(2,1)S(1)} %copy_bitcast_fusion), channel_id=1, replica_groups=mesh['wide'=32,'narrow'=4] {'wide'}, dimensions={1} | all-to-all | bytes 262144 | tf_op jit(solution)/shard_map/all_to_all | solution.py:190
  771.7 0.7 copy.70
  (50 shorter events, 1.4 us)
Async XLA Ops:
  6.5 373.9 %copy-start = (bf16[128,4096]{1,0:T(8,128)(2,1)S(1)}, bf16[128,4096]{1,0:T(8,128)(2,1)}, u32[]{:S(2)}) copy-start(bf16[128,4096]{1,0:T(8,128)(2,1)} %param.19) | copy-start | bytes 3145732
  6.5 125.2 %all-gather.4.cloned.1.call-start = ((), (), s32[]{:S(2)}) async-start(), calls=%async_computation.5 | async-start | bytes 4325376 | tf_op jit(solution)/shard_map/all_gather | solution.py:105
  7.3 532.6 %reduce-scatter.3.cloned.1.call-start = ((), (), s32[]{:S(2)}) async-start(), calls=%async_computation.6 | async-start | bytes 8650752 | tf_op jit(solution)/shard_map/reduce_scatter | solution.py:151
  131.8 3.4 copy-start.2
  131.8 4.7 copy-start.6
  136.5 2.3 copy-start.4
  136.5 4.3 copy-start.5
  138.8 1.9 copy-start.3
  388.5 152.7 %copy-start.7 = (f32[4096]{0:T(1024)S(1)}, f32[4096]{0:T(1024)}, u32[]{:S(2)}) copy-start(f32[4096]{0:T(1024)} %param.22) | copy-start | bytes 49156
  388.6 233.7 %all-gather.6.cloned.1.call-start = ((), (), s32[]{:S(2)}) async-start(), calls=%async_computation.8 | async-start | bytes 5242880 | tf_op jit(solution)/shard_map/all_gather | solution.py:177
  559.0 171.2 %reduce-scatter.5.cloned.1.call-start = ((), (), s32[]{:S(2)}) async-start(), calls=%async_computation.7 | async-start | bytes 10485760 | tf_op jit(solution)/shard_map/reduce_scatter | solution.py:179
  652.5 88.8 %copy-start.8 = (bf16[4096,16]{0,1:T(8,128)(2,1)S(1)}, bf16[4096,16]{0,1:T(8,128)(2,1)}, u32[]{:S(2)}) copy-start(bf16[4096,16]{0,1:T(8,128)(2,1)} %param.23) | copy-start | bytes 393220
  733.8 21.7 %all-to-all-start.1 = ((bf16[32,1,4,4096]{3,2,1,0:T(4,128)(2,1)}), bf16[32,1,4,4096]{3,2,1,0:T(4,128)(2,1)S(1)}, u32[]{:S(2)}, u32[]{:S(2)}) async-start(bf16[32,1,4,4096]{3,2,1,0:T(4,128)(2,1)} %copy.54), calls=%async_computation.3 | async-start | bytes 2097152 | tf_op jit(solution)/shard_map/all_to_all | solution.py:182
  756.1 16.2 %copy-start.1 = (bf16[128,4096]{1,0:T(8,128)(2,1)S(1)}, bf16[128,4096]{1,0:T(8,128)(2,1)}, u32[]{:S(2)}) copy-start(bf16[128,4096]{1,0:T(8,128)(2,1)} %param.19) | copy-start | bytes 3145732
Sparse Core Ops, SparseCore 0:
  8.9 122.8 all-gather.3
  388.7 151.1 reduce-scatter.2
  559.1 63.0 all-gather.5
  652.6 77.5 reduce-scatter.4
where the time goes:
time: 781 us; the launch traced here: 779 us
  waiting for transfers between devices  427 us (55%)
  blocking collectives  253 us (32%)
  matrix products  49.2 us (6%)
  other arithmetic  15.5 us (2%)
  local copies, waits for them, and re-layouts  13.5 us (2%)
  between operations  13.4 us (2%)
    psum x1, blocking collectives, body(): key_cols, value_cols = lax.psum((key_term, value_term), 'wide')  165 us
    reduce_scatter x1, waiting for transfers between devices, body(): lax.psum_scatter(jnp.dot(attended, out_weight, preferred_element_type=jnp...  150 us
    all_gather x1, waiting for transfers between devices, body(): full_rows = lax.all_gather(hidden, 'wide', axis=1, tiled=True)  123 us
    reduce_scatter x1, waiting for transfers between devices, body(): lax.psum_scatter(partial_out, 'narrow', scatter_dimension=0, tiled=True)  77.6 us
    all_gather x1, waiting for transfers between devices, body(): lax.all_gather(arrived, 'narrow', axis=0, tiled=True)  63.2 us
    all_gather x1, blocking collectives, body(): lax.all_gather(fresh_keys, 'narrow', axis=0, tiled=True)  51.3 us
    dot_general x1, matrix products, expert_terms(): jnp.einsum('gscf,sfd->gscd', active, w_down, preferred_element_type=jnp.f...  22.6 us
  transfers between devices with their start and end apart: 5, of which 5 were waited for; matrix products, arithmetic and copies ran while one was open for 1% of the time, Pallas kernels for 0%

commit v1 on v0

v1 whole, which is shorter than its diff:
```python
import jax
import jax.numpy as jnp
from jax import lax
from jax.experimental import pallas as pl
from jax.experimental.pallas import tpu as pltpu
from jax.sharding import PartitionSpec as P

MESH = pl.DeviceIdType.MESH
F32 = jnp.float32
BF16 = jnp.bfloat16

XN, YL, ZN = 4, 2, 4
WIDE = XN * YL * ZN
NARROW = 4
ROWS = 512
LANE = 128
D = WIDE * LANE
HALF = ROWS // 2
KV_SHARE = 4
EXPERTS = 16
CAP = 4
BLOCK = 16
HIDDEN = 800
EPS = 1e-5
SCALE = LANE**-0.5


def remote(src, dst, send_sem, recv_sem, wide, narrow):
    return pltpu.make_async_remote_copy(
        src_ref=src,
        dst_ref=dst,
        send_sem=send_sem,
        recv_sem=recv_sem,
        device_id=(wide, narrow),
        device_id_type=MESH,
    )


def wait_bytes(ref, sem):
    pltpu.make_async_copy(ref, ref, sem).wait()


def dot(a, b):
    return jnp.dot(a, b, preferred_element_type=F32)


def wide_of(x, y, z):
    return (x * YL + y) * ZN + z


class Spread:
    def __init__(self, own, buf, me, narrow, send_sem, recv_sem):
        self.own, self.buf, self.me, self.narrow = own, buf, me, narrow
        self.send_sem, self.recv_sem = send_sem, recv_sem
        self.x = me // (YL * ZN)
        self.y = (me // ZN) % YL
        self.z = me % ZN
        self.started = []

    def place(self, half, first, y, second):
        return wide_of(first, y, second) if half == 0 else wide_of(second, y, first)

    def coordinates(self, half):
        return (self.x, self.z) if half == 0 else (self.z, self.x)

    def send(self, half, block, target):
        rows = pl.ds(half * HALF, HALF)
        own = block is None
        slot = self.me if own else block
        copy = remote(
            self.own.at[rows] if own else self.buf.at[slot, rows],
            self.buf.at[slot, rows],
            self.send_sem.at[len(self.started)],
            self.recv_sem.at[half, slot],
            target,
            self.narrow,
        )
        copy.start()
        self.started.append(copy)

    def arrive(self, half, block):
        rows = pl.ds(half * HALF, HALF)
        wait_bytes(self.buf.at[block, rows], self.recv_sem.at[half, block])

    def around(self, half, block, dimension):
        first, second = self.coordinates(half)
        for step in (1, 3):
            if dimension == 0:
                target = self.place(half, (first + step) % 4, self.y, second)
            else:
                target = self.place(half, first, self.y, (second + step) % 4)
            self.send(half, block, target)

    def start(self):
        for half in (0, 1):
            first, second = self.coordinates(half)
            self.send(half, None, self.place(half, first, 1 - self.y, second))
        for half in (0, 1):
            self.around(half, None, 0)
        for half in (0, 1):
            self.around(half, None, 1)

    def run(self):
        for half in (0, 1):
            first, second = self.coordinates(half)
            block = self.place(half, first, 1 - self.y, second)
            self.arrive(half, block)
            self.around(half, block, 0)
            self.around(half, block, 1)
        for y in (0, 1):
            for step in (1, 3):
                for half in (0, 1):
                    first, second = self.coordinates(half)
                    block = self.place(half, (first + step) % 4, y, second)
                    self.arrive(half, block)
                    if (step == 3) == (y == 0):
                        opposite = (first + 4 - step) % 4
                        self.send(half, block, self.place(half, opposite, self.y, second))
                    self.around(half, block, 1)
        for y in (0, 1):
            for half in (0, 1):
                first, second = self.coordinates(half)
                block = self.place(half, (first + 2) % 4, y, second)
                self.arrive(half, block)
                self.around(half, block, 1)
        for hop in (0, 1, 3, 2):
            for y in (0, 1):
                for step in (1, 3):
                    for half in (0, 1):
                        first, second = self.coordinates(half)
                        block = self.place(half, (first + hop) % 4, y, (second + step) % 4)
                        self.arrive(half, block)
                        if (step == 3) == (y == 0):
                            opposite = (second + 4 - step) % 4
                            self.send(half, block, self.place(half, first, self.y, opposite))
        for hop in (0, 1, 3, 2):
            for y in (0, 1):
                for half in (0, 1):
                    first, second = self.coordinates(half)
                    self.arrive(half, self.place(half, (first + hop) % 4, y, (second + 2) % 4))

    def finish(self):
        for copy in self.started:
            copy.wait_send()


SENDS = 62


def greet(peers):
    barrier = pltpu.get_barrier_semaphore()
    for count, peer in peers:

        def one(i, carry, peer=peer):
            wide, narrow = peer(i)
            pl.semaphore_signal(barrier, inc=1, device_id=(wide, narrow), device_id_type=MESH)
            return carry

        lax.fori_loop(0, count, one, 0)
    pl.semaphore_wait(barrier, sum(count for count, _ in peers))


def attention_kernel(
    hidden,
    gain,
    query_weight,
    key_weight,
    value_weight,
    out_weight,
    cache_key,
    cache_value,
    residual,
    gathered,
    mixed,
    normed,
    joined,
    columns,
    out_columns,
    out_joined,
    kv,
    queries,
    attended,
    own_hidden,
    spread_send,
    spread_recv,
    spread_send2,
    spread_recv2,
    local_sem,
    column_send,
    column_recv,
    pair_sem,
    kv_send,
    kv_recv,
):
    me = lax.axis_index("wide")
    n = lax.axis_index("narrow")
    core = n % 2
    partner = n + 1 - 2 * core
    parity = me % 2
    group = me // KV_SHARE
    mate = me + 1 - 2 * parity

    greet(
        [
            (WIDE - 1, lambda i: ((me + 1 + i) % WIDE, n)),
            (NARROW - 1, lambda i: (me, (n + 1 + i) % NARROW)),
            (NARROW - 1, lambda i: (mate, (n + 1 + i) % NARROW)),
        ]
    )

    spread = Spread(hidden, gathered, me, n, spread_send, spread_recv)
    spread.start()
    locals_ = [
        pltpu.make_async_copy(hidden, gathered.at[me], local_sem.at[0]),
        pltpu.make_async_copy(query_weight, joined.at[:, pl.ds(0, LANE)], local_sem.at[1]),
        pltpu.make_async_copy(cache_key.at[group], kv.at[0, 0], local_sem.at[2]),
        pltpu.make_async_copy(cache_value.at[group], kv.at[1, 0], local_sem.at[3]),
        pltpu.make_async_copy(hidden, own_hidden, local_sem.at[4]),
    ]
    for copy in locals_:
        copy.start()

    half_rows = pl.ds(core * (LANE // 2), LANE // 2)

    def send_column(i, carry):
        target = (me + 1 + i) % WIDE
        cut = pl.ds(pl.multiple_of((target // KV_SHARE) * LANE, LANE), LANE)

        @pl.when(target % 2 == 0)
        def _():
            remote(
                key_weight.at[half_rows, cut], columns.at[core, me], column_send.at[0], column_recv.at[0], target, n
            ).start()

        @pl.when(target % 2 == 1)
        def _():
            remote(
                value_weight.at[half_rows, cut], columns.at[core, me], column_send.at[0], column_recv.at[0], target, n
            ).start()

        return carry

    lax.fori_loop(0, WIDE - 1, send_column, 0)
    own_cut = pl.ds(pl.multiple_of(group * LANE, LANE), LANE)

    @pl.when(parity == 0)
    def _():
        pltpu.make_async_copy(key_weight.at[half_rows, own_cut], columns.at[core, me], local_sem.at[5]).start()

    @pl.when(parity == 1)
    def _():
        pltpu.make_async_copy(value_weight.at[half_rows, own_cut], columns.at[core, me], local_sem.at[5]).start()

    spread.run()

    wait_bytes(columns.at[core, me], local_sem.at[5])
    wait_bytes(columns.at[0, pl.ds(0, WIDE - 1)], column_recv.at[0])
    swap = remote(columns.at[core], columns.at[core], pair_sem.at[0], pair_sem.at[1], me, partner)
    swap.start()

    def send_out_column(i, carry):
        target = (me + 1 + i) % WIDE
        cut = pl.ds(pl.multiple_of(target * LANE, LANE), LANE)
        remote(
            out_weight.at[half_rows, cut], out_columns.at[core, me], column_send.at[1], column_recv.at[1], target, n
        ).start()
        return carry

    lax.fori_loop(0, WIDE - 1, send_out_column, 0)
    own_out = pltpu.make_async_copy(
        out_weight.at[half_rows, pl.ds(pl.multiple_of(me * LANE, LANE), LANE)], out_columns.at[core, me], local_sem.at[6]
    )
    own_out.start()

    for copy in locals_:
        copy.wait()

    swap.wait()
    for half in (0, 1):
        for w in range(WIDE):
            joined[w * LANE + half * (LANE // 2) : w * LANE + (half + 1) * (LANE // 2), LANE:] = columns[half, w]

    def project(tile, carry):
        rows = pl.ds(pl.multiple_of(tile * LANE, LANE), LANE)
        total = jnp.zeros((LANE, LANE), F32)
        for w in range(WIDE):
            total += gathered[w, rows].astype(F32)
        average = jnp.sum(total, axis=1, keepdims=True) * (1.0 / D)
        total = jnp.zeros((LANE, LANE), F32)
        for w in range(WIDE):
            centered = gathered[w, rows].astype(F32) - average
            total += centered * centered
        scale = lax.rsqrt(jnp.sum(total, axis=1, keepdims=True) * (1.0 / D) + EPS)
        for w in range(WIDE):
            centered = gathered[w, rows].astype(F32) - average
            normed[:, w * LANE : (w + 1) * LANE] = (centered * scale * gain[w : w + 1, :]).astype(BF16)
        product = dot(normed[...], joined[...]).astype(BF16)
        queries[rows] = product[:, :LANE]
        kv[parity, n + 1, rows] = product[:, LANE:]
        return carry

    lax.fori_loop(0, ROWS // LANE, project, 0)

    for other in range(NARROW):

        @pl.when(other > n)
        def _():
            block = kv.at[parity, n + 1]
            remote(block, block, kv_send.at[0, other], kv_recv.at[parity, n], me, other).start()

        @pl.when(other >= n)
        def _():
            block = kv.at[parity, n + 1]
            remote(block, block, kv_send.at[1, other], kv_recv.at[parity, n], mate, other).start()

    for other in range(NARROW):

        @pl.when(other < n)
        def _():
            wait_bytes(kv.at[parity, other + 1], kv_recv.at[parity, other])

        @pl.when(other <= n)
        def _():
            wait_bytes(kv.at[1 - parity, other + 1], kv_recv.at[1 - parity, other])

    tile_rows = HALF

    def attend(tile, carry):
        rows = pl.ds(pl.multiple_of(tile * tile_rows, tile_rows), tile_rows)
        q = queries[rows]
        row_ids = tile * tile_rows + lax.broadcasted_iota(jnp.int32, (tile_rows, ROWS), 0)
        key_ids = lax.broadcasted_iota(jnp.int32, (tile_rows, ROWS), 1)
        causal = key_ids <= row_ids

        def block(j, state):
            highest, total, acc = state
            scores = (
                lax.dot_general(q, kv[0, j], (((1,), (1,)), ((), ())), preferred_element_type=F32) * SCALE
            )
            scores = jnp.where(jnp.logical_or(causal, j <= n), scores, -1e30)
            new = jnp.maximum(highest, jnp.max(scores, axis=1, keepdims=True))
            weights = jnp.exp(scores - new)
            fade = jnp.exp(highest - new)
            total = total * fade + jnp.sum(weights, axis=1, keepdims=True)
            acc = acc * fade + dot(weights.astype(BF16), kv[1, j])
            return new, total, acc

        start = (
            jnp.full((tile_rows, 1), -1e30, F32),
            jnp.zeros((tile_rows, 1), F32),
            jnp.zeros((tile_rows, LANE), F32),
        )
        _, total, acc = lax.fori_loop(0, n + 2, block, start)
        attended[rows] = (acc / total).astype(BF16)
        return carry

    lax.fori_loop(0, ROWS // tile_rows, attend, 0)

    spread2 = Spread(attended, mixed, me, n, spread_send2, spread_recv2)
    spread2.start()
    own_mixed = pltpu.make_async_copy(attended, mixed.at[me], local_sem.at[7])
    own_mixed.start()
    own_out.wait()
    wait_bytes(out_columns.at[0, pl.ds(0, WIDE - 1)], column_recv.at[1])
    swap_out = remote(out_columns.at[core], out_columns.at[core], pair_sem.at[2], pair_sem.at[3], me, partner)
    swap_out.start()
    spread2.run()
    swap_out.wait()
    for half in (0, 1):
        for w in range(WIDE):
            out_joined[w * LANE + half * (LANE // 2) : w * LANE + (half + 1) * (LANE // 2), :] = out_columns[half, w]
    own_mixed.wait()

    def mix(tile, carry):
        rows = pl.ds(pl.multiple_of(tile * LANE, LANE), LANE)
        total = own_hidden[rows].astype(F32)
        product = jnp.zeros((LANE, LANE), F32)
        for w in range(0, WIDE, 2):
            pair = jnp.concatenate([mixed[w, rows], mixed[w + 1, rows]], axis=1)
            product += dot(pair, out_joined[w * LANE : (w + 2) * LANE, :])
        residual[rows] = (total + product).astype(BF16)
        return carry

    lax.fori_loop(0, ROWS // LANE, mix, 0)

    spread.finish()
    spread2.finish()
    for which in range(2):
        wait_bytes(columns.at[0, pl.ds(0, WIDE - 1)], column_send.at[which])
    for other in range(NARROW):

        @pl.when(other > n)
        def _():
            wait_bytes(kv.at[parity, n + 1], kv_send.at[0, other])

        @pl.when(other >= n)
        def _():
            wait_bytes(kv.at[parity, n + 1], kv_send.at[1, other])


GROUPS = ROWS // LANE
GROUP_SLOTS = LANE // BLOCK * CAP
COLS = 512
STEPS = D // COLS


def expert_kernel(
    residual,
    gain,
    router,
    ids,
    gate_weight,
    up_weight,
    down_weight,
    result,
    gate,
    up,
    down,
    stats,
    stats_in,
    diffs,
    diffs_in,
    normed,
    outgoing,
    arrived,
    tokens,
    active,
    partial_out,
    partial_in,
    returning,
    returned,
    weight_sem,
    small_send,
    small_recv,
    local_sem,
    out_send,
    out_recv,
    pair_send,
    pair_recv,
    partial_send,
    partial_recv,
    back_send,
    back_recv,
):
    me = lax.axis_index("wide")
    n = lax.axis_index("narrow")
    core = n % 2
    high = n // 2
    partner = n + 1 - 2 * core
    far = n + 2 - 4 * high

    loads = [
        pltpu.make_async_copy(gate_weight.at[0], gate, weight_sem.at[0]),
        pltpu.make_async_copy(up_weight.at[0], up, weight_sem.at[1]),
        pltpu.make_async_copy(down_weight.at[0], down, weight_sem.at[2]),
    ]
    for load in loads:
        load.start()

    greet(
        [
            (WIDE - 1, lambda i: ((me + 1 + i) % WIDE, n)),
            (WIDE, lambda i: ((me + i) % WIDE, far)),
            (1, lambda i: (me, partner)),
        ]
    )

    eye = (
        lax.broadcasted_iota(jnp.int32, (LANE, LANE), 0) == lax.broadcasted_iota(jnp.int32, (LANE, LANE), 1)
    ).astype(F32)

    def to_row(column):
        return jnp.sum(column * eye, axis=0, keepdims=True)

    def to_column(row):
        return jnp.sum(row * eye, axis=1, keepdims=True)

    def share(mine, everyone, which):
        def one(i, carry):
            target = (me + 1 + i) % WIDE
            remote(mine, everyone.at[me], small_send.at[which], small_recv.at[which], target, n).start()
            return carry

        lax.fori_loop(0, WIDE - 1, one, 0)

    def collect(mine, everyone, which):
        everyone[me] = mine[...]
        wait_bytes(everyone.at[pl.ds(0, WIDE - 1)], small_recv.at[which])

    for g in range(GROUPS):
        values = residual[g * LANE : (g + 1) * LANE].astype(F32)
        average = jnp.sum(values, axis=1, keepdims=True) * (1.0 / LANE)
        centered = values - average
        spread_of = jnp.sum(centered * centered, axis=1, keepdims=True)
        stats[g : g + 1, :] = to_row(average)
        stats[GROUPS + g : GROUPS + g + 1, :] = to_row(spread_of)
    share(stats, stats_in, 0)

    below = lax.broadcasted_iota(jnp.int32, (LANE, LANE), 0)
    left = lax.broadcasted_iota(jnp.int32, (LANE, LANE), 1)
    earlier = jnp.logical_and(left < below, left // BLOCK == below // BLOCK).astype(BF16)
    expert_ids = lax.broadcasted_iota(jnp.int32, (LANE, EXPERTS), 1)
    slot_ids = lax.broadcasted_iota(jnp.int32, (LANE, EXPERTS * GROUP_SLOTS), 1)
    in_group = lax.broadcasted_iota(jnp.int32, (LANE, 1), 0) // BLOCK * CAP

    def chosen(g):
        pair = ids[g * LANE : (g + 1) * LANE, :]
        return [expert_ids == pair[:, k : k + 1] for k in (0, 1)]

    def placing(g):
        pair = ids[g * LANE : (g + 1) * LANE, :]
        hot = chosen(g)
        before = dot(earlier, jnp.logical_or(hot[0], hot[1]).astype(BF16))
        found = []
        for k in (0, 1):
            position = jnp.sum(jnp.where(hot[k], before, 0.0), axis=1, keepdims=True).astype(jnp.int32)
            slot = pair[:, k : k + 1] * GROUP_SLOTS + in_group + position
            found.append((slot_ids == slot).astype(BF16))
        return found

    collect(stats, stats_in, 0)
    averages = jnp.zeros((GROUPS, LANE), F32)
    for w in range(WIDE):
        averages += stats_in[w, :GROUPS]
    averages = averages * (1.0 / WIDE)
    squares = jnp.zeros((GROUPS, LANE), F32)
    for w in range(WIDE):
        shift = stats_in[w, :GROUPS] - averages
        squares += stats_in[w, GROUPS:] + LANE * (shift * shift)
    scales = lax.rsqrt(squares * (1.0 / D) + EPS)
    own_gain = gain[pl.ds(me, 1), :]
    own_router = router[me]
    for g in range(GROUPS):
        values = residual[g * LANE : (g + 1) * LANE].astype(F32)
        here = (
            (values - to_column(averages[g : g + 1])) * to_column(scales[g : g + 1]) * own_gain
        ).astype(BF16)
        first, second = placing(g)
        filled = lax.dot_general(
            first + second, here, (((0,), (0,)), ((), ())), preferred_element_type=F32
        ).astype(BF16)
        outgoing[:, g * GROUP_SLOTS : (g + 1) * GROUP_SLOTS, :] = filled.reshape(EXPERTS, GROUP_SLOTS, LANE)
        normed[g * LANE : (g + 1) * LANE] = here

    def dispatch(i, carry):
        target = (me + i) % WIDE

        @pl.when(i > 0)
        def _():
            remote(
                outgoing.at[target // 2], arrived.at[n * WIDE + me], out_send.at[0], out_recv.at[n // 2], target, n
            ).start()

        remote(
            outgoing.at[target // 2], arrived.at[n * WIDE + me], out_send.at[0], out_recv.at[n // 2], target, far
        ).start()
        return carry

    lax.fori_loop(0, WIDE, dispatch, 0)
    own_chunk = pltpu.make_async_copy(outgoing.at[me // 2], arrived.at[n * WIDE + me], local_sem.at[0])
    own_chunk.start()

    for g in range(GROUPS):
        hot = chosen(g)
        logits = dot(normed[g * LANE : (g + 1) * LANE], own_router)
        lead = jnp.sum(jnp.where(hot[0], logits, 0.0) - jnp.where(hot[1], logits, 0.0), axis=1, keepdims=True)
        diffs[g : g + 1, :] = to_row(lead)
        diffs[GROUPS + g : GROUPS + g + 1, :] = jnp.zeros((1, LANE), F32)
    share(diffs, diffs_in, 1)

    own_chunk.wait()
    wait_bytes(arrived.at[pl.ds(0, WIDE - 1)], out_recv.at[high])
    swaps = []
    for where in (high, 1 - high):
        if where is not high:
            wait_bytes(arrived.at[pl.ds(0, WIDE)], out_recv.at[where])
        part = arrived.at[pl.ds((where * 2 + core) * WIDE, WIDE)]
        swap = remote(part, part, pair_send.at[where], pair_recv.at[where], me, partner)
        swap.start()
        swaps.append(swap)
    collect(diffs, diffs_in, 1)
    for swap in swaps:
        swap.wait_send()
    for where in (0, 1):
        wait_bytes(arrived.at[pl.ds(0, WIDE)], pair_recv.at[where])
    for load in loads:
        load.wait()

    def hidden_units(which):
        for where in (0, 1):
            for w in range(WIDE):
                tokens[where * LANE : (where + 1) * LANE, w * LANE : (w + 1) * LANE] = arrived[
                    (where * 2 + which) * WIDE + w
                ]
        gated = dot(tokens[...], gate[...])
        raised = dot(tokens[...], up[...])
        active[...] = (gated / (1.0 + jnp.exp(-gated)) * raised).astype(BF16)

    hidden_units(1 - core)

    def give(step, carry):
        cut = pl.ds(pl.multiple_of(step * COLS, COLS), COLS)
        partial_out[step] = dot(active[...], down[:, cut]).astype(BF16)
        remote(
            partial_out.at[step], partial_in.at[step], partial_send.at[step], partial_recv.at[step], me, partner
        ).start()
        return carry

    lax.fori_loop(0, STEPS, give, 0)
    hidden_units(core)

    def keep(step, carry):
        cut = pl.ds(pl.multiple_of(step * COLS, COLS), COLS)
        wait_bytes(partial_in.at[step], partial_recv.at[step])
        total = (dot(active[...], down[:, cut]) + partial_in[step].astype(F32)).astype(BF16)
        for where in (0, 1):
            for k in range(COLS // LANE):
                target = step * (COLS // LANE) + k
                slot = where * WIDE + target
                returning[slot] = total[where * LANE : (where + 1) * LANE, k * LANE : (k + 1) * LANE]
                own = jnp.logical_and(target == me, where == high)

                @pl.when(jnp.logical_not(own))
                def _():
                    remote(
                        returning.at[slot],
                        returned.at[high * WIDE + me],
                        back_send.at[0],
                        back_recv.at[high],
                        target,
                        where * 2 + core,
                    ).start()

                @pl.when(own)
                def _():
                    pltpu.make_async_copy(
                        returning.at[slot], returned.at[high * WIDE + me], local_sem.at[1]
                    ).start()

        return carry

    lax.fori_loop(0, STEPS, keep, 0)

    leads = jnp.zeros((GROUPS, LANE), F32)
    for w in range(WIDE):
        leads += diffs_in[w, :GROUPS]
    heavy = 1.0 / (1.0 + jnp.exp(-leads))
    wait_bytes(returned.at[0], local_sem.at[1])
    wait_bytes(returned.at[pl.ds(0, WIDE - 1)], back_recv.at[high])
    wait_bytes(returned.at[pl.ds(0, WIDE)], back_recv.at[1 - high])
    for g in range(GROUPS):
        first, second = placing(g)
        picks = [jnp.zeros((LANE, LANE), F32)] * 2
        for where in (0, 1):
            for s in (0, 1):
                rows = jnp.concatenate(
                    [
                        returned[where * WIDE + 2 * e + s, g * GROUP_SLOTS : (g + 1) * GROUP_SLOTS, :]
                        for e in range(EXPERTS)
                    ],
                    axis=0,
                )
                picks = [picks[0] + dot(first, rows), picks[1] + dot(second, rows)]
        weight = to_column(heavy[g : g + 1])
        result[g * LANE : (g + 1) * LANE] = (
            residual[g * LANE : (g + 1) * LANE].astype(F32) + weight * picks[0] + (1.0 - weight) * picks[1]
        ).astype(BF16)

    for which in (0, 1):
        wait_bytes(stats_in.at[pl.ds(0, WIDE - 1)], small_send.at[which])
    wait_bytes(arrived.at[pl.ds(0, 2 * WIDE - 1)], out_send.at[0])
    wait_bytes(returned.at[pl.ds(0, 2 * WIDE - 1)], back_send.at[0])
    for step in range(STEPS):
        wait_bytes(partial_out.at[step], partial_send.at[step])


def body(
    hidden,
    attn_gain,
    query_weight,
    key_weight,
    value_weight,
    out_weight,
    cache_key,
    cache_value,
    mlp_gain,
    router_weight,
    expert_ids,
    gate_weight,
    up_weight,
    down_weight,
):
    anywhere = pl.BlockSpec(memory_space=pl.ANY)
    vmem = pl.BlockSpec(memory_space=pltpu.VMEM)
    dma = pltpu.SemaphoreType.DMA
    residual = pl.pallas_call(
        attention_kernel,
        out_shape=jax.ShapeDtypeStruct((ROWS, LANE), BF16),
        in_specs=[anywhere, vmem] + [anywhere] * 6,
        out_specs=vmem,
        scratch_shapes=[
            pltpu.VMEM((WIDE, ROWS, LANE), BF16),
            pltpu.VMEM((WIDE, ROWS, LANE), BF16),
            pltpu.VMEM((LANE, D), BF16),
            pltpu.VMEM((D, 2 * LANE), BF16),
            pltpu.VMEM((2, WIDE, LANE // 2, LANE), BF16),
            pltpu.VMEM((2, WIDE, LANE // 2, LANE), BF16),
            pltpu.VMEM((D, LANE), BF16),
            pltpu.VMEM((2, NARROW + 1, ROWS, LANE), BF16),
            pltpu.VMEM((ROWS, LANE), BF16),
            pltpu.VMEM((ROWS, LANE), BF16),
            pltpu.VMEM((ROWS, LANE), BF16),
            dma((SENDS,)),
            dma((2, WIDE)),
            dma((SENDS,)),
            dma((2, WIDE)),
            dma((8,)),
            dma((2,)),
            dma((2,)),
            dma((4,)),
            dma((2, NARROW)),
            dma((2, NARROW)),
        ],
        compiler_params=pltpu.CompilerParams(
            collective_id=0, has_side_effects=True, vmem_limit_bytes=56 * 2**20
        ),
    )(
        hidden,
        attn_gain.reshape(WIDE, LANE),
        query_weight,
        key_weight,
        value_weight,
        out_weight,
        cache_key,
        cache_value,
    )
    return pl.pallas_call(
        expert_kernel,
        out_shape=jax.ShapeDtypeStruct((ROWS, LANE), BF16),
        in_specs=[vmem] * 4 + [anywhere] * 3,
        out_specs=vmem,
        scratch_shapes=[
            pltpu.VMEM((D, HIDDEN), BF16),
            pltpu.VMEM((D, HIDDEN), BF16),
            pltpu.VMEM((HIDDEN, D), BF16),
            pltpu.VMEM((2 * GROUPS, LANE), F32),
            pltpu.VMEM((WIDE, 2 * GROUPS, LANE), F32),
            pltpu.VMEM((2 * GROUPS, LANE), F32),
            pltpu.VMEM((WIDE, 2 * GROUPS, LANE), F32),
            pltpu.VMEM((ROWS, LANE), BF16),
            pltpu.VMEM((EXPERTS, LANE, LANE), BF16),
            pltpu.VMEM((NARROW * WIDE, LANE, LANE), BF16),
            pltpu.VMEM((2 * LANE, D), BF16),
            pltpu.VMEM((2 * LANE, HIDDEN), BF16),
            pltpu.VMEM((STEPS, 2 * LANE, COLS), BF16),
            pltpu.VMEM((STEPS, 2 * LANE, COLS), BF16),
            pltpu.VMEM((2 * WIDE, LANE, LANE), BF16),
            pltpu.VMEM((2 * WIDE, LANE, LANE), BF16),
            dma((3,)),
            dma((2,)),
            dma((2,)),
            dma((2,)),
            dma((1,)),
            dma((2,)),
            dma((2,)),
            dma((2,)),
            dma((STEPS,)),
            dma((STEPS,)),
            dma((1,)),
            dma((2,)),
        ],
        compiler_params=pltpu.CompilerParams(
            collective_id=1, has_side_effects=True, vmem_limit_bytes=56 * 2**20
        ),
    )(
        residual,
        mlp_gain.reshape(WIDE, LANE),
        router_weight.reshape(WIDE, LANE, EXPERTS),
        expert_ids,
        gate_weight,
        up_weight,
        down_weight,
    )


def solution(mesh):
    placed = (
        P("narrow", "wide"),
        P(),
        P(None, "wide"),
        P("wide", None),
        P("wide", None),
        P("wide", None),
        P(),
        P(),
        P(),
        P(),
        P("narrow", None),
        P("wide", None, "narrow"),
        P("wide", None, "narrow"),
        P("wide", "narrow", None),
    )
    return jax.shard_map(
        body, mesh=mesh, in_specs=placed, out_specs=P("narrow", "wide"), check_vma=False
    )
```

time: 781 us -> 230 us (0.29)
  the two profiles are of different devices: /device:TPU:1 before, /device:TPU:127 now
where the time goes in v1:
time: 230 us; the launch traced here: 229 us
  Pallas kernels  202 us (88%)
  local copies, waits for them, and re-layouts  26.4 us (11%)
    pallas_call x1, Pallas kernels, body(): pl.pallas_call(expert_kernel, out_shape=jax.ShapeDtypeStruct((ROWS, LANE)...  116 us
    pallas_call x1, Pallas kernels, body(): pl.pallas_call(attention_kernel, out_shape=jax.ShapeDtypeStruct((ROWS, LA...  86.5 us
    unnamed x5, local copies, waits for them, and re-layouts  26.4 us

profile of v1, /device:TPU:127, one launch (start us, length us, event | category | flops | bytes accessed | tf_op | source)
XLA Modules:
  0.0 228.8 jit_solution(9359889160670003314)
XLA Ops:
  0.0 86.5 %shard_map.136.residual = bf16[512,128]{1,0:T(8,128)(2,1)} custom-call(bf16[512,128]{1,0:T(8,128)(2,1)} %hidden.1, f32[32,128]{1,0:T(8,128)} %bitcast.4, bf16[4096,128]{1,0:T(8,128)(2,1)} %query_weight.1, bf16[128,1024]{1,0:T(8,128)(2,1)} %key_weight.1, bf16[128,1024]{1,0:T(8,128)(2,1)} %value_weight.1, bf16[128,4096]{1,0:T(8,128)(2,1)} %out_weight.1, ...), custom_call_target="tpu_custom_call" | custom-call | tf_op jit(solution)/shard_map/pallas_call | solution.py:696
  86.5 1.5 copy.16.ids
  88.0 2.2 copy.15
  90.2 10.5 %copy.17.gate_weight = bf16[1,4096,800]{2,1,0:T(8,128)(2,1)} copy(bf16[1,4096,800]{1,2,0:T(8,128)(2,1)} %param.25) | data formatting | bytes 13107200 | tf_op args[11]
  100.8 10.6 %copy.18.up_weight = bf16[1,4096,800]{2,1,0:T(8,128)(2,1)} copy(bf16[1,4096,800]{1,2,0:T(8,128)(2,1)} %param.26) | data formatting | bytes 13107200 | tf_op args[12]
  111.3 115.9 %shard_map.137 = bf16[512,128]{1,0:T(8,128)(2,1)} custom-call(bf16[512,128]{1,0:T(8,128)(2,1)} %shard_map.136.residual, f32[32,128]{1,0:T(8,128)} %bitcast.5, bf16[32,128,16]{2,1,0:T(8,128)(2,1)} %bitcast.3, s32[512,2]{1,0:T(8,128)} %copy.16.ids, bf16[1,4096,800]{2,1,0:T(8,128)(2,1)} %copy.17.gate_weight, bf16[1,4096,800]{2,1,0:T(8,128)(2,1)} %copy.18.up_weight, ...), custom_call_target="tpu_custom_call" | custom-call | tf_op jit(solution)/shard_map/pallas_call | solution.py:737
  227.3 1.6 copy.20

commit v2 on v1

v2 whole, which is shorter than its diff:
```python
import jax
import jax.numpy as jnp
from jax import lax
from jax.experimental import pallas as pl
from jax.experimental.pallas import tpu as pltpu
from jax.sharding import PartitionSpec as P

MESH = pl.DeviceIdType.MESH
F32 = jnp.float32
BF16 = jnp.bfloat16

XN, YL, ZN = 4, 2, 4
WIDE = XN * YL * ZN
NARROW = 4
ROWS = 512
LANE = 128
D = WIDE * LANE
HALF = ROWS // 2
KV_SHARE = 4
EXPERTS = 16
CAP = 4
BLOCK = 16
HIDDEN = 800
EPS = 1e-5
SCALE = LANE**-0.5


def remote(src, dst, send_sem, recv_sem, wide, narrow):
    return pltpu.make_async_remote_copy(
        src_ref=src,
        dst_ref=dst,
        send_sem=send_sem,
        recv_sem=recv_sem,
        device_id=(wide, narrow),
        device_id_type=MESH,
    )


def wait_bytes(ref, sem):
    pltpu.make_async_copy(ref, ref, sem).wait()


def dot(a, b):
    return jnp.dot(a, b, preferred_element_type=F32)


def wide_of(x, y, z):
    return (x * YL + y) * ZN + z


def flipped(index, mask, bits):
    return sum(((index // 2**b + mask // 2**b) % 2) * 2**b for b in range(bits))


class Spread:
    def __init__(self, own, buf, me, narrow, send_sem, recv_sem):
        self.own, self.buf, self.me, self.narrow = own, buf, me, narrow
        self.send_sem, self.recv_sem = send_sem, recv_sem
        self.x = me // (YL * ZN)
        self.y = (me // ZN) % YL
        self.z = me % ZN
        self.started = []

    def place(self, half, first, y, second):
        return wide_of(first, y, second) if half == 0 else wide_of(second, y, first)

    def coordinates(self, half):
        return (self.x, self.z) if half == 0 else (self.z, self.x)

    def send(self, half, block, target):
        rows = pl.ds(half * HALF, HALF)
        own = block is None
        slot = self.me if own else block
        copy = remote(
            self.own.at[rows] if own else self.buf.at[slot, rows],
            self.buf.at[slot, rows],
            self.send_sem.at[len(self.started)],
            self.recv_sem.at[half, slot],
            target,
            self.narrow,
        )
        copy.start()
        self.started.append(copy)

    def arrive(self, half, block):
        rows = pl.ds(half * HALF, HALF)
        wait_bytes(self.buf.at[block, rows], self.recv_sem.at[half, block])

    def around(self, half, block, dimension):
        first, second = self.coordinates(half)
        for step in (1, 3):
            if dimension == 0:
                target = self.place(half, (first + step) % 4, self.y, second)
            else:
                target = self.place(half, first, self.y, (second + step) % 4)
            self.send(half, block, target)

    def start(self):
        for half in (0, 1):
            first, second = self.coordinates(half)
            self.send(half, None, self.place(half, first, 1 - self.y, second))
        for half in (0, 1):
            self.around(half, None, 0)
        for half in (0, 1):
            self.around(half, None, 1)

    def run(self):
        for half in (0, 1):
            first, second = self.coordinates(half)
            block = self.place(half, first, 1 - self.y, second)
            self.arrive(half, block)
            self.around(half, block, 0)
            self.around(half, block, 1)
        for y in (0, 1):
            for step in (1, 3):
                for half in (0, 1):
                    first, second = self.coordinates(half)
                    block = self.place(half, (first + step) % 4, y, second)
                    self.arrive(half, block)
                    if (step == 3) == (y == 0):
                        opposite = (first + 4 - step) % 4
                        self.send(half, block, self.place(half, opposite, self.y, second))
                    self.around(half, block, 1)
        for y in (0, 1):
            for half in (0, 1):
                first, second = self.coordinates(half)
                block = self.place(half, (first + 2) % 4, y, second)
                self.arrive(half, block)
                self.around(half, block, 1)
        for hop in (0, 1, 3, 2):
            for y in (0, 1):
                for step in (1, 3):
                    for half in (0, 1):
                        first, second = self.coordinates(half)
                        block = self.place(half, (first + hop) % 4, y, (second + step) % 4)
                        self.arrive(half, block)
                        if (step == 3) == (y == 0):
                            opposite = (second + 4 - step) % 4
                            self.send(half, block, self.place(half, first, self.y, opposite))
        for hop in (0, 1, 3, 2):
            for y in (0, 1):
                for half in (0, 1):
                    first, second = self.coordinates(half)
                    self.arrive(half, self.place(half, (first + hop) % 4, y, (second + 2) % 4))

    def finish(self):
        for copy in self.started:
            copy.wait_send()


SENDS = 62


def greet(peers):
    barrier = pltpu.get_barrier_semaphore()
    for count, peer in peers:

        def one(i, carry, peer=peer):
            wide, narrow = peer(i)
            pl.semaphore_signal(barrier, inc=1, device_id=(wide, narrow), device_id_type=MESH)
            return carry

        lax.fori_loop(0, count, one, 0)
    pl.semaphore_wait(barrier, sum(count for count, _ in peers))


GROUPS = ROWS // LANE
GROUP_SLOTS = LANE // BLOCK * CAP
PART = LANE // 2
COLS = 512
STEPS = D // COLS
LAG = 2
BITS = 5
ALL = NARROW * WIDE


def dot_t(a, b):
    return lax.dot_general(a, b, (((1,), (1,)), ((), ())), preferred_element_type=F32)


def layer_kernel(
    hidden,
    gain,
    query_weight,
    key_weight,
    value_weight,
    out_weight,
    cache_key,
    cache_value,
    gain_two,
    router,
    ids,
    gate_weight,
    up_weight,
    down_weight,
    result,
    gathered,
    mixed,
    normed,
    joined,
    columns,
    out_columns,
    out_joined,
    kv,
    queries,
    attended,
    own_hidden,
    residual,
    gate,
    up,
    down,
    stats,
    stats_in,
    diffs,
    diffs_in,
    placed,
    outgoing,
    arrived,
    tokens,
    active,
    partial_out,
    partial_in,
    kept,
    returning,
    returned,
    spread_send,
    spread_recv,
    spread_send2,
    spread_recv2,
    local_sem,
    column_send,
    column_recv,
    pair_sem,
    kv_send,
    kv_recv,
    weight_sem,
    small_send,
    small_recv,
    out_send,
    out_recv,
    pair_send,
    pair_recv,
    partial_send,
    partial_recv,
    back_send,
    back_recv,
):
    me = lax.axis_index("wide")
    n = lax.axis_index("narrow")
    core = n % 2
    high = n // 2
    partner = n + 1 - 2 * core
    far = n + 2 - 4 * high
    across = far + 1 - 2 * core
    parity = me % 2
    group = me // KV_SHARE
    mate = me + 1 - 2 * parity

    locals_ = [
        pltpu.make_async_copy(hidden, gathered.at[me], local_sem.at[0]),
        pltpu.make_async_copy(query_weight, joined.at[:, pl.ds(0, LANE)], local_sem.at[1]),
        pltpu.make_async_copy(cache_key.at[group], kv.at[0, 0], local_sem.at[2]),
        pltpu.make_async_copy(cache_value.at[group], kv.at[1, 0], local_sem.at[3]),
        pltpu.make_async_copy(hidden, own_hidden, local_sem.at[4]),
    ]
    for copy in locals_:
        copy.start()
    loads = [
        pltpu.make_async_copy(gate_weight.at[0], gate, weight_sem.at[0]),
        pltpu.make_async_copy(up_weight.at[0], up, weight_sem.at[1]),
        pltpu.make_async_copy(down_weight.at[0], down, weight_sem.at[2]),
    ]

    greet(
        [
            (WIDE - 1, lambda i: ((me + 1 + i) % WIDE, n)),
            (WIDE, lambda i: ((me + i) % WIDE, far)),
            (2, lambda i: (me, partner + i * (across - partner))),
            (2, lambda i: (mate, partner + i * (across - partner))),
        ]
    )

    spread = Spread(hidden, gathered, me, n, spread_send, spread_recv)
    spread.start()

    half_rows = pl.ds(core * (LANE // 2), LANE // 2)

    def send_column(i, carry):
        target = flipped(me, i + 1, BITS)
        cut = pl.ds(pl.multiple_of((target // KV_SHARE) * LANE, LANE), LANE)

        @pl.when(target % 2 == 0)
        def _():
            remote(
                key_weight.at[half_rows, cut], columns.at[core, me], column_send.at[0], column_recv.at[0], target, n
            ).start()

        @pl.when(target % 2 == 1)
        def _():
            remote(
                value_weight.at[half_rows, cut], columns.at[core, me], column_send.at[0], column_recv.at[0], target, n
            ).start()

        return carry

    lax.fori_loop(0, WIDE - 1, send_column, 0)
    own_cut = pl.ds(pl.multiple_of(group * LANE, LANE), LANE)

    @pl.when(parity == 0)
    def _():
        pltpu.make_async_copy(key_weight.at[half_rows, own_cut], columns.at[core, me], local_sem.at[5]).start()

    @pl.when(parity == 1)
    def _():
        pltpu.make_async_copy(value_weight.at[half_rows, own_cut], columns.at[core, me], local_sem.at[5]).start()

    spread.run()
    for load in loads:
        load.start()

    wait_bytes(columns.at[core, me], local_sem.at[5])
    wait_bytes(columns.at[0, pl.ds(0, WIDE - 1)], column_recv.at[0])
    swap = remote(columns.at[core], columns.at[core], pair_sem.at[0], pair_sem.at[1], me, partner)
    swap.start()

    def send_out_column(i, carry):
        target = flipped(me, i + 1, BITS)
        cut = pl.ds(pl.multiple_of(target * LANE, LANE), LANE)
        remote(
            out_weight.at[half_rows, cut], out_columns.at[core, me], column_send.at[1], column_recv.at[1], target, n
        ).start()
        return carry

    lax.fori_loop(0, WIDE - 1, send_out_column, 0)
    own_out = pltpu.make_async_copy(
        out_weight.at[half_rows, pl.ds(pl.multiple_of(me * LANE, LANE), LANE)], out_columns.at[core, me], local_sem.at[6]
    )
    own_out.start()

    for copy in locals_:
        copy.wait()

    swap.wait()
    for half in (0, 1):
        for w in range(WIDE):
            joined[w * LANE + half * (LANE // 2) : w * LANE + (half + 1) * (LANE // 2), LANE:] = columns[half, w]

    def project(tile, carry):
        rows = pl.ds(pl.multiple_of(tile * LANE, LANE), LANE)
        total = jnp.zeros((LANE, LANE), F32)
        for w in range(WIDE):
            total += gathered[w, rows].astype(F32)
        average = jnp.sum(total, axis=1, keepdims=True) * (1.0 / D)
        total = jnp.zeros((LANE, LANE), F32)
        for w in range(WIDE):
            centered = gathered[w, rows].astype(F32) - average
            total += centered * centered
        scale = lax.rsqrt(jnp.sum(total, axis=1, keepdims=True) * (1.0 / D) + EPS)
        for w in range(WIDE):
            centered = gathered[w, rows].astype(F32) - average
            normed[:, w * LANE : (w + 1) * LANE] = (centered * scale * gain[w : w + 1, :]).astype(BF16)
        product = dot(normed[...], joined[...]).astype(BF16)
        queries[rows] = product[:, :LANE]
        kv[parity, n + 1, rows] = product[:, LANE:]
        return carry

    def fresh(kind, block, half):
        return kv.at[kind, block + 1, pl.ds(half * HALF, HALF)]

    for half in (0, 1):
        lax.fori_loop(half * 2, half * 2 + 2, project, 0)
        for other in range(NARROW):

            @pl.when(other >= n)
            def _():
                block = fresh(parity, n, half)
                remote(block, block, kv_send.at[1, half, other], kv_recv.at[parity, half, n], mate, other).start()

            @pl.when(other > n)
            def _():
                block = fresh(parity, n, half)
                remote(block, block, kv_send.at[0, half, other], kv_recv.at[parity, half, n], me, other).start()

    row_ids = lax.broadcasted_iota(jnp.int32, (ROWS, ROWS), 0)
    key_ids = lax.broadcasted_iota(jnp.int32, (ROWS, ROWS), 1)
    causal = key_ids <= row_ids

    def attend(j, state):
        highest, total, acc = state
        scores = dot_t(queries[...], kv[0, j]) * SCALE
        scores = jnp.where(jnp.logical_or(causal, j <= n), scores, -1e30)
        new = jnp.maximum(highest, jnp.max(scores, axis=1, keepdims=True))
        weights = jnp.exp(scores - new)
        fade = jnp.exp(highest - new)
        total = total * fade + jnp.sum(weights, axis=1, keepdims=True)
        acc = acc * fade + dot(weights.astype(BF16), kv[1, j])
        return new, total, acc

    state = (
        jnp.full((ROWS, 1), -1e30, F32),
        jnp.zeros((ROWS, 1), F32),
        jnp.zeros((ROWS, LANE), F32),
    )
    state = lax.fori_loop(0, 1, attend, state)
    for half in (0, 1):
        for other in range(NARROW):

            @pl.when(other < n)
            def _():
                wait_bytes(fresh(parity, other, half), kv_recv.at[parity, half, other])

            @pl.when(other <= n)
            def _():
                wait_bytes(fresh(1 - parity, other, half), kv_recv.at[1 - parity, half, other])

    _, total, acc = lax.fori_loop(1, n + 2, attend, state)
    attended[...] = (acc / total).astype(BF16)

    spread2 = Spread(attended, mixed, me, n, spread_send2, spread_recv2)
    spread2.start()
    own_mixed = pltpu.make_async_copy(attended, mixed.at[me], local_sem.at[7])
    own_mixed.start()
    own_out.wait()
    wait_bytes(out_columns.at[0, pl.ds(0, WIDE - 1)], column_recv.at[1])
    swap_out = remote(out_columns.at[core], out_columns.at[core], pair_sem.at[2], pair_sem.at[3], me, partner)
    swap_out.start()

    eye = (
        lax.broadcasted_iota(jnp.int32, (LANE, LANE), 0) == lax.broadcasted_iota(jnp.int32, (LANE, LANE), 1)
    ).astype(F32)

    def to_row(column):
        return jnp.sum(column * eye, axis=0, keepdims=True)

    def to_column(row):
        return jnp.sum(row * eye, axis=1, keepdims=True)

    below = lax.broadcasted_iota(jnp.int32, (LANE, LANE), 0)
    left = lax.broadcasted_iota(jnp.int32, (LANE, LANE), 1)
    earlier = jnp.logical_and(left < below, left // BLOCK == below // BLOCK).astype(BF16)
    expert_ids = lax.broadcasted_iota(jnp.int32, (LANE, EXPERTS), 1)
    slot_ids = lax.broadcasted_iota(jnp.int32, (LANE, EXPERTS * GROUP_SLOTS), 1)
    in_group = lax.broadcasted_iota(jnp.int32, (LANE, 1), 0) // BLOCK * CAP

    def named(g):
        return [
            to_column(ids[k : k + 1, g * LANE : (g + 1) * LANE].astype(F32)).astype(jnp.int32) for k in (0, 1)
        ]

    for g in range(GROUPS):
        pair = named(g)
        hot = [expert_ids == chosen for chosen in pair]
        before = dot(earlier, jnp.logical_or(hot[0], hot[1]).astype(BF16))
        for k in (0, 1):
            position = jnp.sum(jnp.where(hot[k], before, 0.0), axis=1, keepdims=True).astype(jnp.int32)
            slot = pair[k] * GROUP_SLOTS + in_group + position
            placed[g, k] = (slot_ids == slot).astype(BF16)

    spread2.run()
    swap_out.wait()
    for half in (0, 1):
        for w in range(WIDE):
            out_joined[w * LANE + half * (LANE // 2) : w * LANE + (half + 1) * (LANE // 2), :] = out_columns[half, w]
    own_mixed.wait()

    def dispatch(part):
        def one(i, carry):
            target = flipped(me, i, BITS)
            source = outgoing.at[part, target // 2]
            slot = arrived.at[part * ALL + n * WIDE + me]

            @pl.when(i > 0)
            def _():
                remote(source, slot, out_send.at[part], out_recv.at[part, high], target, n).start()

            remote(source, slot, out_send.at[part], out_recv.at[part, high], target, far).start()
            return carry

        lax.fori_loop(0, WIDE, one, 0)
        pltpu.make_async_copy(
            outgoing.at[part, me // 2], arrived.at[part * ALL + n * WIDE + me], local_sem.at[8 + part]
        ).start()

    def share(mine, everyone, which):
        def one(i, carry):
            target = flipped(me, i + 1, BITS)
            remote(mine, everyone.at[me], small_send.at[which], small_recv.at[which], target, n).start()
            return carry

        lax.fori_loop(0, WIDE - 1, one, 0)

    def collect(mine, everyone, which):
        everyone[me] = mine[...]
        wait_bytes(everyone.at[pl.ds(0, WIDE - 1)], small_recv.at[which])

    for part in (0, 1):
        for g in (2 * part, 2 * part + 1):
            rows = slice(g * LANE, (g + 1) * LANE)
            product = jnp.zeros((LANE, LANE), F32)
            for w in range(0, WIDE, 2):
                pair = jnp.concatenate([mixed[w, rows], mixed[w + 1, rows]], axis=1)
                product += dot(pair, out_joined[w * LANE : (w + 2) * LANE, :])
            here = (own_hidden[rows].astype(F32) + product).astype(BF16)
            residual[rows] = here
            filled = lax.dot_general(
                placed[g, 0] + placed[g, 1], here, (((0,), (0,)), ((), ())), preferred_element_type=F32
            ).astype(BF16)
            at = (g % 2) * GROUP_SLOTS
            outgoing[part, :, at : at + GROUP_SLOTS, :] = filled.reshape(EXPERTS, GROUP_SLOTS, LANE)
        dispatch(part)

    for g in range(GROUPS):
        values = residual[g * LANE : (g + 1) * LANE].astype(F32)
        average = jnp.sum(values, axis=1, keepdims=True) * (1.0 / LANE)
        centered = values - average
        deviations = jnp.sum(centered * centered, axis=1, keepdims=True)
        stats[g : g + 1, :] = to_row(average)
        stats[GROUPS + g : GROUPS + g + 1, :] = to_row(deviations)
    share(stats, stats_in, 0)

    def norm_tokens(part, source):
        base = part * ALL + source * WIDE
        total = jnp.zeros((PART, LANE), F32)
        for w in range(WIDE):
            total += arrived[base + w].astype(F32)
        average = jnp.sum(total, axis=1, keepdims=True) * (1.0 / D)
        total = jnp.zeros((PART, LANE), F32)
        for w in range(WIDE):
            centered = arrived[base + w].astype(F32) - average
            total += centered * centered
        scale = lax.rsqrt(jnp.sum(total, axis=1, keepdims=True) * (1.0 / D) + EPS)
        where = pl.ds(pl.multiple_of((source % 2) * LANE + (source // 2) * PART, PART), PART)
        for w in range(WIDE):
            centered = arrived[base + w].astype(F32) - average
            tokens[where, w * LANE : (w + 1) * LANE] = (centered * scale * gain_two[w : w + 1, :]).astype(BF16)

    def receive(part):
        wait_bytes(outgoing.at[part, 0], local_sem.at[8 + part])
        swaps = []
        for order, where in enumerate((high, 1 - high)):
            count = WIDE - 1 if order == 0 else WIDE
            wait_bytes(arrived.at[pl.ds(0, count)], out_recv.at[part, where])
            piece = arrived.at[pl.ds(part * ALL + (where * 2 + core) * WIDE, WIDE)]
            swap = remote(piece, piece, pair_send.at[part, where], pair_recv.at[part, where], me, partner)
            swap.start()
            swaps.append(swap)
        return swaps

    def experts(part):
        for where in (0, 1):
            norm_tokens(part, where * 2 + core)
        for where in (0, 1):
            wait_bytes(arrived.at[pl.ds(0, WIDE)], pair_recv.at[part, where])
            norm_tokens(part, where * 2 + 1 - core)
        gated = dot_t(tokens[...], gate[...])
        raised = dot_t(tokens[...], up[...])
        active[...] = (gated / (1.0 + jnp.exp(-gated)) * raised).astype(BF16)

        def step(k, carry):
            @pl.when(k < STEPS)
            def _():
                block = flipped(me // 4, k, 3)
                cut = pl.ds(pl.multiple_of(block * COLS, COLS), COLS)
                total = dot(active[...], down[:, cut])

                @pl.when(core == 0)
                def _():
                    kept[k] = total[:LANE]
                    partial_out[part * STEPS + k] = total[LANE:].astype(BF16)

                @pl.when(core == 1)
                def _():
                    kept[k] = total[LANE:]
                    partial_out[part * STEPS + k] = total[:LANE].astype(BF16)

                at = part * STEPS + k
                remote(
                    partial_out.at[at], partial_in.at[at], partial_send.at[at], partial_recv.at[at], me, partner
                ).start()

            @pl.when(k >= LAG)
            def _():
                late = k - LAG
                block = flipped(me // 4, late, 3)
                at = part * STEPS + late
                wait_bytes(partial_in.at[at], partial_recv.at[at])
                total = (kept[late] + partial_in[at].astype(F32)).astype(BF16)
                base = part * 2 * WIDE + block * 4
                for where in (0, 1):
                    for q in range(4):
                        returning[base + where * WIDE + q] = total[
                            where * PART : (where + 1) * PART, q * LANE : (q + 1) * LANE
                        ]
                for q in range(4):
                    spot = flipped(me % 4, q, 2)
                    target = block * 4 + spot
                    for turn in (0, 1):
                        where = high if turn == 0 else 1 - high
                        slot = returning.at[base + where * WIDE + spot]
                        home = returned.at[part * 2 * WIDE + high * WIDE + me]
                        sems = back_send.at[part], back_recv.at[part, high]
                        if turn == 1 or q > 0:
                            remote(slot, home, *sems, target, where * 2 + core).start()
                        else:

                            @pl.when(late > 0)
                            def _():
                                remote(slot, home, *sems, target, where * 2 + core).start()

                            @pl.when(late == 0)
                            def _():
                                pltpu.make_async_copy(slot, home, local_sem.at[10 + part]).start()

            return carry

        lax.fori_loop(0, STEPS + LAG, step, 0)

    def combine(part):
        wait_bytes(returned.at[0], local_sem.at[10 + part])
        wait_bytes(returned.at[pl.ds(0, WIDE - 1)], back_recv.at[part, high])
        wait_bytes(returned.at[pl.ds(0, WIDE)], back_recv.at[part, 1 - high])
        for g in (2 * part, 2 * part + 1):
            at = (g % 2) * GROUP_SLOTS
            picks = [jnp.zeros((LANE, LANE), F32)] * 2
            for where in (0, 1):
                for s in (0, 1):
                    rows = jnp.concatenate(
                        [
                            returned[(part * 2 + where) * WIDE + 2 * e + s, at : at + GROUP_SLOTS, :]
                            for e in range(EXPERTS)
                        ],
                        axis=0,
                    )
                    picks = [picks[k] + dot(placed[g, k], rows) for k in (0, 1)]
            weight = to_column(heavy[g : g + 1])
            result[g * LANE : (g + 1) * LANE] = (
                residual[g * LANE : (g + 1) * LANE].astype(F32) + weight * picks[0] + (1.0 - weight) * picks[1]
            ).astype(BF16)

    swaps = receive(0)

    collect(stats, stats_in, 0)
    averages = jnp.zeros((GROUPS, LANE), F32)
    for w in range(WIDE):
        averages += stats_in[w, :GROUPS]
    averages = averages * (1.0 / WIDE)
    squares = jnp.zeros((GROUPS, LANE), F32)
    for w in range(WIDE):
        shift = stats_in[w, :GROUPS] - averages
        squares += stats_in[w, GROUPS:] + LANE * (shift * shift)
    scales = lax.rsqrt(squares * (1.0 / D) + EPS)
    own_gain = gain_two[pl.ds(me, 1), :]
    own_router = router[:, pl.ds(pl.multiple_of(me * LANE, LANE), LANE)]
    for g in range(GROUPS):
        values = residual[g * LANE : (g + 1) * LANE].astype(F32)
        here = ((values - to_column(averages[g : g + 1])) * to_column(scales[g : g + 1]) * own_gain).astype(BF16)
        logits = dot_t(here, own_router)
        pair = named(g)
        lead = jnp.sum(
            jnp.where(expert_ids == pair[0], logits, 0.0) - jnp.where(expert_ids == pair[1], logits, 0.0),
            axis=1,
            keepdims=True,
        )
        diffs[g : g + 1, :] = to_row(lead)
        diffs[GROUPS + g : GROUPS + g + 1, :] = jnp.zeros((1, LANE), F32)
    share(diffs, diffs_in, 1)

    for load in loads:
        load.wait()
    experts(0)
    swaps += receive(1)
    experts(1)

    collect(diffs, diffs_in, 1)
    leads = jnp.zeros((GROUPS, LANE), F32)
    for w in range(WIDE):
        leads += diffs_in[w, :GROUPS]
    heavy = 1.0 / (1.0 + jnp.exp(-leads))
    combine(0)
    combine(1)

    spread.finish()
    spread2.finish()
    for swap in swaps:
        swap.wait_send()
    for which in range(2):
        wait_bytes(columns.at[0, pl.ds(0, WIDE - 1)], column_send.at[which])
        wait_bytes(stats_in.at[pl.ds(0, WIDE - 1)], small_send.at[which])
        wait_bytes(arrived.at[pl.ds(0, 2 * WIDE - 1)], out_send.at[which])
        wait_bytes(returned.at[pl.ds(0, 2 * WIDE - 1)], back_send.at[which])
    for half in (0, 1):
        for other in range(NARROW):

            @pl.when(other > n)
            def _():
                wait_bytes(fresh(parity, n, half), kv_send.at[0, half, other])

            @pl.when(other >= n)
            def _():
                wait_bytes(fresh(parity, n, half), kv_send.at[1, half, other])

    for at in range(2 * STEPS):
        wait_bytes(partial_out.at[at], partial_send.at[at])


def body(
    hidden,
    attn_gain,
    query_weight,
    key_weight,
    value_weight,
    out_weight,
    cache_key,
    cache_value,
    mlp_gain,
    router_weight,
    expert_ids,
    gate_weight,
    up_weight,
    down_weight,
):
    anywhere = pl.BlockSpec(memory_space=pl.ANY)
    vmem = pl.BlockSpec(memory_space=pltpu.VMEM)
    dma = pltpu.SemaphoreType.DMA

    def held(*shape, kind=BF16):
        return pltpu.VMEM(shape, kind)

    return pl.pallas_call(
        layer_kernel,
        out_shape=jax.ShapeDtypeStruct((ROWS, LANE), BF16),
        in_specs=[anywhere, vmem] + [anywhere] * 6 + [vmem] * 3 + [anywhere] * 3,
        out_specs=vmem,
        scratch_shapes=[
            held(WIDE, ROWS, LANE),
            held(WIDE, ROWS, LANE),
            held(LANE, D),
            held(D, 2 * LANE),
            held(2, WIDE, LANE // 2, LANE),
            held(2, WIDE, LANE // 2, LANE),
            held(D, LANE),
            held(2, NARROW + 1, ROWS, LANE),
            held(ROWS, LANE),
            held(ROWS, LANE),
            held(ROWS, LANE),
            held(ROWS, LANE),
            held(HIDDEN, D),
            held(HIDDEN, D),
            held(HIDDEN, D),
            held(2 * GROUPS, LANE, kind=F32),
            held(WIDE, 2 * GROUPS, LANE, kind=F32),
            held(2 * GROUPS, LANE, kind=F32),
            held(WIDE, 2 * GROUPS, LANE, kind=F32),
            held(GROUPS, 2, LANE, EXPERTS * GROUP_SLOTS),
            held(2, EXPERTS, PART, LANE),
            held(2 * ALL, PART, LANE),
            held(2 * LANE, D),
            held(2 * LANE, HIDDEN),
            held(2 * STEPS, LANE, COLS),
            held(2 * STEPS, LANE, COLS),
            held(STEPS, LANE, COLS, kind=F32),
            held(4 * WIDE, PART, LANE),
            held(4 * WIDE, PART, LANE),
            dma((SENDS,)),
            dma((2, WIDE)),
            dma((SENDS,)),
            dma((2, WIDE)),
            dma((12,)),
            dma((2,)),
            dma((2,)),
            dma((4,)),
            dma((2, 2, NARROW)),
            dma((2, 2, NARROW)),
            dma((3,)),
            dma((2,)),
            dma((2,)),
            dma((2,)),
            dma((2, 2)),
            dma((2, 2)),
            dma((2, 2)),
            dma((2 * STEPS,)),
            dma((2 * STEPS,)),
            dma((2,)),
            dma((2, 2)),
        ],
        compiler_params=pltpu.CompilerParams(
            collective_id=0, has_side_effects=True, vmem_limit_bytes=60 * 2**20
        ),
    )(
        hidden,
        attn_gain.reshape(WIDE, LANE),
        query_weight,
        key_weight,
        value_weight,
        out_weight,
        cache_key,
        cache_value,
        mlp_gain.reshape(WIDE, LANE),
        router_weight.T,
        expert_ids.T,
        gate_weight.swapaxes(1, 2),
        up_weight.swapaxes(1, 2),
        down_weight,
    )


def solution(mesh):
    placed = (
        P("narrow", "wide"),
        P(),
        P(None, "wide"),
        P("wide", None),
        P("wide", None),
        P("wide", None),
        P(),
        P(),
        P(),
        P(),
        P("narrow", None),
        P("wide", None, "narrow"),
        P("wide", None, "narrow"),
        P("wide", "narrow", None),
    )
    return jax.shard_map(
        body, mesh=mesh, in_specs=placed, out_specs=P("narrow", "wide"), check_vma=False
    )
```

time: 230 us -> 166 us (0.72)
  the two profiles are of different devices: /device:TPU:127 before, /device:TPU:1 now
where the time goes in v2:
time: 166 us
  Pallas kernels  164 us (99%)
    pallas_call x1, Pallas kernels, body(): pl.pallas_call(layer_kernel, out_shape=jax.ShapeDtypeStruct((ROWS, LANE),...  164 us

profile of v2, /device:TPU:1, one launch (start us, length us, event | category | flops | bytes accessed | tf_op | source)
XLA Modules:
  0.0 166.0 jit_solution(15166126706191179999)
XLA Ops:
  0.0 164.4 %shard_map.136 = bf16[512,128]{1,0:T(8,128)(2,1)} custom-call(bf16[512,128]{1,0:T(8,128)(2,1)} %hidden.1, f32[32,128]{1,0:T(8,128)} %bitcast.9, bf16[4096,128]{1,0:T(8,128)(2,1)} %query_weight.1, bf16[128,1024]{1,0:T(8,128)(2,1)} %key_weight.1, bf16[128,1024]{1,0:T(8,128)(2,1)} %value_weight.1, bf16[128,4096]{1,0:T(8,128)(2,1)} %out_weight.1, ...), custom_call_target="tpu_custom_call" | custom-call | tf_op jit(solution)/shard_map/pallas_call | solution.py:729
  164.4 1.6 copy.16

commit v3 on v2

--- a/solution.py
+++ b/solution.py
@@ -53,8 +53,9 @@
 
 
 class Spread:
-    def __init__(self, own, buf, me, narrow, send_sem, recv_sem):
+    def __init__(self, own, buf, me, narrow, send_sem, recv_sem, begin, visit):
         self.own, self.buf, self.me, self.narrow = own, buf, me, narrow
+        self.begin, self.visit = begin, visit
         self.send_sem, self.recv_sem = send_sem, recv_sem
         self.x = me // (YL * ZN)
         self.y = (me // ZN) % YL
@@ -111,6 +112,10 @@
             self.arrive(half, block)
             self.around(half, block, 0)
             self.around(half, block, 1)
+        self.begin()
+        for half in (0, 1):
+            first, second = self.coordinates(half)
+            self.visit(self.place(half, first, 1 - self.y, second), half)
         for y in (0, 1):
             for step in (1, 3):
                 for half in (0, 1):
@@ -121,12 +126,14 @@
                         opposite = (first + 4 - step) % 4
                         self.send(half, block, self.place(half, opposite, self.y, second))
                     self.around(half, block, 1)
+                    self.visit(block, half)
         for y in (0, 1):
             for half in (0, 1):
                 first, second = self.coordinates(half)
                 block = self.place(half, (first + 2) % 4, y, second)
                 self.arrive(half, block)
                 self.around(half, block, 1)
+                self.visit(block, half)
         for hop in (0, 1, 3, 2):
             for y in (0, 1):
                 for step in (1, 3):
@@ -137,11 +144,14 @@
                         if (step == 3) == (y == 0):
                             opposite = (second + 4 - step) % 4
                             self.send(half, block, self.place(half, first, self.y, opposite))
+                        self.visit(block, half)
         for hop in (0, 1, 3, 2):
             for y in (0, 1):
                 for half in (0, 1):
                     first, second = self.coordinates(half)
-                    self.arrive(half, self.place(half, (first + hop) % 4, y, (second + 2) % 4))
+                    block = self.place(half, (first + hop) % 4, y, (second + 2) % 4)
+                    self.arrive(half, block)
+                    self.visit(block, half)
 
     def finish(self):
         for copy in self.started:
@@ -166,7 +176,8 @@
 
 GROUPS = ROWS // LANE
 GROUP_SLOTS = LANE // BLOCK * CAP
-PART = LANE // 2
+PARTS = ((0, 2), (2, 1), (3, 1))
+OWN = 2 * GROUP_SLOTS
 COLS = 512
 STEPS = D // COLS
 LAG = 2
@@ -206,6 +217,9 @@
     attended,
     own_hidden,
     residual,
+    shift,
+    sums,
+    mixture,
     gate,
     up,
     down,
@@ -280,7 +294,21 @@
         ]
     )
 
-    spread = Spread(hidden, gathered, me, n, spread_send, spread_recv)
+    def gather_own():
+        locals_[4].wait()
+        own = own_hidden[...].astype(F32)
+        shift[...] = jnp.broadcast_to(jnp.sum(own, axis=1, keepdims=True) * (1.0 / LANE), (ROWS, LANE))
+        own = own - shift[...]
+        sums[0] = own
+        sums[1] = own * own
+
+    def gather_sums(block, half):
+        rows = slice(half * HALF, (half + 1) * HALF)
+        moved = gathered[block, rows].astype(F32) - shift[rows]
+        sums[0, rows] += moved
+        sums[1, rows] += moved * moved
+
+    spread = Spread(hidden, gathered, me, n, spread_send, spread_recv, gather_own, gather_sums)
     spread.start()
 
     half_rows = pl.ds(core * (LANE // 2), LANE // 2)
@@ -337,7 +365,7 @@
     )
     own_out.start()
 
-    for copy in locals_:
+    for copy in locals_[:4]:
         copy.wait()
 
     swap.wait()
@@ -347,15 +375,10 @@
 
     def project(tile, carry):
         rows = pl.ds(pl.multiple_of(tile * LANE, LANE), LANE)
-        total = jnp.zeros((LANE, LANE), F32)
-        for w in range(WIDE):
-            total += gathered[w, rows].astype(F32)
-        average = jnp.sum(total, axis=1, keepdims=True) * (1.0 / D)
-        total = jnp.zeros((LANE, LANE), F32)
-        for w in range(WIDE):
-            centered = gathered[w, rows].astype(F32) - average
-            total += centered * centered
-        scale = lax.rsqrt(jnp.sum(total, axis=1, keepdims=True) * (1.0 / D) + EPS)
+        offset = jnp.sum(sums[0, rows], axis=1, keepdims=True) * (1.0 / D)
+        square = jnp.sum(sums[1, rows], axis=1, keepdims=True) * (1.0 / D)
+        average = jnp.max(shift[rows], axis=1, keepdims=True) + offset
+        scale = lax.rsqrt(jnp.maximum(square - offset * offset, 0.0) + EPS)
         for w in range(WIDE):
             centered = gathered[w, rows].astype(F32) - average
             normed[:, w * LANE : (w + 1) * LANE] = (centered * scale * gain[w : w + 1, :]).astype(BF16)
@@ -367,19 +390,25 @@
     def fresh(kind, block, half):
         return kv.at[kind, block + 1, pl.ds(half * HALF, HALF)]
 
+    def give(kind, half, block, order, wide, narrow):
+        piece = fresh(kind, block, half)
+        remote(piece, piece, kv_send.at[half, order], kv_recv.at[kind, half, block], wide, narrow).start()
+
+    def take(kind, half, block):
+        wait_bytes(fresh(kind, block, half), kv_recv.at[kind, half, block])
+
     for half in (0, 1):
         lax.fori_loop(half * 2, half * 2 + 2, project, 0)
-        for other in range(NARROW):
-
-            @pl.when(other >= n)
-            def _():
-                block = fresh(parity, n, half)
-                remote(block, block, kv_send.at[1, half, other], kv_recv.at[parity, half, n], mate, other).start()
-
-            @pl.when(other > n)
-            def _():
-                block = fresh(parity, n, half)
-                remote(block, block, kv_send.at[0, half, other], kv_recv.at[parity, half, n], me, other).start()
+        give(parity, half, n, 0, mate, n)
+
+        @pl.when(high == 0)
+        def _():
+            give(parity, half, n, 1, me, far)
+            give(parity, half, n, 2, mate, far)
+
+        @pl.when(core == 0)
+        def _():
+            give(parity, half, n, 3, me, partner)
 
     row_ids = lax.broadcasted_iota(jnp.int32, (ROWS, ROWS), 0)
     key_ids = lax.broadcasted_iota(jnp.int32, (ROWS, ROWS), 1)
@@ -402,28 +431,23 @@
         jnp.zeros((ROWS, LANE), F32),
     )
     state = lax.fori_loop(0, 1, attend, state)
-    for half in (0, 1):
-        for other in range(NARROW):
-
-            @pl.when(other < n)
-            def _():
-                wait_bytes(fresh(parity, other, half), kv_recv.at[parity, half, other])
-
-            @pl.when(other <= n)
-            def _():
-                wait_bytes(fresh(1 - parity, other, half), kv_recv.at[1 - parity, half, other])
-
-    _, total, acc = lax.fori_loop(1, n + 2, attend, state)
-    attended[...] = (acc / total).astype(BF16)
-
-    spread2 = Spread(attended, mixed, me, n, spread_send2, spread_recv2)
-    spread2.start()
-    own_mixed = pltpu.make_async_copy(attended, mixed.at[me], local_sem.at[7])
-    own_mixed.start()
     own_out.wait()
     wait_bytes(out_columns.at[0, pl.ds(0, WIDE - 1)], column_recv.at[1])
     swap_out = remote(out_columns.at[core], out_columns.at[core], pair_sem.at[2], pair_sem.at[3], me, partner)
     swap_out.start()
+    for half in (0, 1):
+        take(1 - parity, half, n)
+
+        @pl.when(core == 0)
+        def _():
+            give(1 - parity, half, n, 4, me, partner)
+
+        @pl.when(high == 1)
+        def _():
+            take(parity, half, far)
+            give(parity, half, far, 5, me, partner)
+            take(1 - parity, half, far)
+            give(1 - parity, half, far, 6, me, partner)
 
     eye = (
         lax.broadcasted_iota(jnp.int32, (LANE, LANE), 0) == lax.broadcasted_iota(jnp.int32, (LANE, LANE), 1)
@@ -456,18 +480,48 @@
             slot = pair[k] * GROUP_SLOTS + in_group + position
             placed[g, k] = (slot_ids == slot).astype(BF16)
 
-    spread2.run()
     swap_out.wait()
     for half in (0, 1):
         for w in range(WIDE):
             out_joined[w * LANE + half * (LANE // 2) : w * LANE + (half + 1) * (LANE // 2), :] = out_columns[half, w]
-    own_mixed.wait()
+
+    for half in (0, 1):
+
+        @pl.when(core == 1)
+        def _():
+            take(parity, half, partner)
+            take(1 - parity, half, partner)
+
+        @pl.when(high == 1)
+        def _():
+            take(parity, half, across)
+            take(1 - parity, half, across)
+
+    _, total, acc = lax.fori_loop(1, n + 2, attend, state)
+    attended[...] = (acc / total).astype(BF16)
+
+    def out_rows(block):
+        return out_joined[pl.ds(pl.multiple_of(block * LANE, LANE), LANE), :]
+
+    def mix_own():
+        mixture[...] = own_hidden[...].astype(F32) + dot(attended[...], out_rows(me))
+
+    def gather_products(block, half):
+        rows = slice(half * HALF, (half + 1) * HALF)
+        mixture[rows] += dot(mixed[block, rows], out_rows(block))
+
+    spread2 = Spread(attended, mixed, me, n, spread_send2, spread_recv2, mix_own, gather_products)
+    spread2.start()
+
+    spread2.run()
 
     def dispatch(part):
+        groups = pl.ds(*PARTS[part])
+        slot = arrived.at[n * WIDE + me, groups]
+
         def one(i, carry):
             target = flipped(me, i, BITS)
-            source = outgoing.at[part, target // 2]
-            slot = arrived.at[part * ALL + n * WIDE + me]
+            source = outgoing.at[target // 2, groups]
 
             @pl.when(i > 0)
             def _():
@@ -477,9 +531,7 @@
             return carry
 
         lax.fori_loop(0, WIDE, one, 0)
-        pltpu.make_async_copy(
-            outgoing.at[part, me // 2], arrived.at[part * ALL + n * WIDE + me], local_sem.at[8 + part]
-        ).start()
+        pltpu.make_async_copy(outgoing.at[me // 2, groups], slot, local_sem.at[8 + part]).start()
 
     def share(mine, everyone, which):
         def one(i, carry):
@@ -493,111 +545,126 @@
         everyone[me] = mine[...]
         wait_bytes(everyone.at[pl.ds(0, WIDE - 1)], small_recv.at[which])
 
-    for part in (0, 1):
-        for g in (2 * part, 2 * part + 1):
-            rows = slice(g * LANE, (g + 1) * LANE)
-            product = jnp.zeros((LANE, LANE), F32)
-            for w in range(0, WIDE, 2):
-                pair = jnp.concatenate([mixed[w, rows], mixed[w + 1, rows]], axis=1)
-                product += dot(pair, out_joined[w * LANE : (w + 2) * LANE, :])
-            here = (own_hidden[rows].astype(F32) + product).astype(BF16)
-            residual[rows] = here
-            filled = lax.dot_general(
-                placed[g, 0] + placed[g, 1], here, (((0,), (0,)), ((), ())), preferred_element_type=F32
-            ).astype(BF16)
-            at = (g % 2) * GROUP_SLOTS
-            outgoing[part, :, at : at + GROUP_SLOTS, :] = filled.reshape(EXPERTS, GROUP_SLOTS, LANE)
-        dispatch(part)
-
-    for g in range(GROUPS):
+    def deviations_of(g):
         values = residual[g * LANE : (g + 1) * LANE].astype(F32)
         average = jnp.sum(values, axis=1, keepdims=True) * (1.0 / LANE)
         centered = values - average
         deviations = jnp.sum(centered * centered, axis=1, keepdims=True)
         stats[g : g + 1, :] = to_row(average)
         stats[GROUPS + g : GROUPS + g + 1, :] = to_row(deviations)
-    share(stats, stats_in, 0)
+
+    for part, (first_group, count) in enumerate(PARTS):
+        for g in range(first_group, first_group + count):
+            rows = slice(g * LANE, (g + 1) * LANE)
+            here = mixture[rows].astype(BF16)
+            residual[rows] = here
+            filled = lax.dot_general(
+                placed[g, 0] + placed[g, 1], here, (((0,), (0,)), ((), ())), preferred_element_type=F32
+            ).astype(BF16)
+            outgoing[:, g] = filled.reshape(EXPERTS, GROUP_SLOTS, LANE)
+        dispatch(part)
+        if part == 0:
+            for g in range(GROUPS):
+                residual[g * LANE : (g + 1) * LANE] = mixture[g * LANE : (g + 1) * LANE].astype(BF16)
+                deviations_of(g)
+            share(stats, stats_in, 0)
 
     def norm_tokens(part, source):
-        base = part * ALL + source * WIDE
-        total = jnp.zeros((PART, LANE), F32)
+        first_group, count = PARTS[part]
+        size = count * GROUP_SLOTS
+
+        def values(w):
+            block = arrived[source * WIDE + w, first_group : first_group + count]
+            return block.reshape(size, LANE).astype(F32)
+
+        total = jnp.zeros((size, LANE), F32)
         for w in range(WIDE):
-            total += arrived[base + w].astype(F32)
+            total += values(w)
         average = jnp.sum(total, axis=1, keepdims=True) * (1.0 / D)
-        total = jnp.zeros((PART, LANE), F32)
+        total = jnp.zeros((size, LANE), F32)
         for w in range(WIDE):
-            centered = arrived[base + w].astype(F32) - average
+            centered = values(w) - average
             total += centered * centered
         scale = lax.rsqrt(jnp.sum(total, axis=1, keepdims=True) * (1.0 / D) + EPS)
-        where = pl.ds(pl.multiple_of((source % 2) * LANE + (source // 2) * PART, PART), PART)
+        where = pl.ds(pl.multiple_of(((source % 2) * 2 + source // 2) * size, GROUP_SLOTS), size)
         for w in range(WIDE):
-            centered = arrived[base + w].astype(F32) - average
+            centered = values(w) - average
             tokens[where, w * LANE : (w + 1) * LANE] = (centered * scale * gain_two[w : w + 1, :]).astype(BF16)
 
+    swaps = []
+
     def receive(part):
-        wait_bytes(outgoing.at[part, 0], local_sem.at[8 + part])
-        swaps = []
+        groups = pl.ds(*PARTS[part])
+        wait_bytes(outgoing.at[0, groups], local_sem.at[8 + part])
         for order, where in enumerate((high, 1 - high)):
-            count = WIDE - 1 if order == 0 else WIDE
-            wait_bytes(arrived.at[pl.ds(0, count)], out_recv.at[part, where])
-            piece = arrived.at[pl.ds(part * ALL + (where * 2 + core) * WIDE, WIDE)]
+            blocks = WIDE - 1 if order == 0 else WIDE
+            wait_bytes(arrived.at[pl.ds(0, blocks), groups], out_recv.at[part, where])
+            piece = arrived.at[pl.ds((where * 2 + core) * WIDE, WIDE), groups]
             swap = remote(piece, piece, pair_send.at[part, where], pair_recv.at[part, where], me, partner)
             swap.start()
             swaps.append(swap)
-        return swaps
 
     def experts(part):
+        first_group, count = PARTS[part]
+        groups = pl.ds(first_group, count)
+        size = count * GROUP_SLOTS
+        rows = count * OWN
+        everything = pl.ds(0, 2 * rows)
         for where in (0, 1):
             norm_tokens(part, where * 2 + core)
         for where in (0, 1):
-            wait_bytes(arrived.at[pl.ds(0, WIDE)], pair_recv.at[part, where])
+            wait_bytes(arrived.at[pl.ds(0, WIDE), groups], pair_recv.at[part, where])
             norm_tokens(part, where * 2 + 1 - core)
-        gated = dot_t(tokens[...], gate[...])
-        raised = dot_t(tokens[...], up[...])
-        active[...] = (gated / (1.0 + jnp.exp(-gated)) * raised).astype(BF16)
+        gated = dot_t(tokens[everything], gate[...])
+        raised = dot_t(tokens[everything], up[...])
+        active[everything] = (gated / (1.0 + jnp.exp(-gated)) * raised).astype(BF16)
+        if part + 1 < len(PARTS):
+            receive(part + 1)
 
         def step(k, carry):
             @pl.when(k < STEPS)
             def _():
                 block = flipped(me // 4, k, 3)
                 cut = pl.ds(pl.multiple_of(block * COLS, COLS), COLS)
-                total = dot(active[...], down[:, cut])
+                total = dot(active[everything], down[:, cut])
+                at = pl.ds(first_group * STEPS + k * count, count)
 
                 @pl.when(core == 0)
                 def _():
-                    kept[k] = total[:LANE]
-                    partial_out[part * STEPS + k] = total[LANE:].astype(BF16)
+                    kept[k, :rows] = total[:rows]
+                    partial_out[at] = total[rows:].astype(BF16).reshape(count, OWN, COLS)
 
                 @pl.when(core == 1)
                 def _():
-                    kept[k] = total[LANE:]
-                    partial_out[part * STEPS + k] = total[:LANE].astype(BF16)
-
-                at = part * STEPS + k
+                    kept[k, :rows] = total[rows:]
+                    partial_out[at] = total[:rows].astype(BF16).reshape(count, OWN, COLS)
+
+                sem = part * STEPS + k
                 remote(
-                    partial_out.at[at], partial_in.at[at], partial_send.at[at], partial_recv.at[at], me, partner
+                    partial_out.at[at], partial_in.at[at], partial_send.at[sem], partial_recv.at[sem], me, partner
                 ).start()
 
             @pl.when(k >= LAG)
             def _():
                 late = k - LAG
                 block = flipped(me // 4, late, 3)
-                at = part * STEPS + late
-                wait_bytes(partial_in.at[at], partial_recv.at[at])
-                total = (kept[late] + partial_in[at].astype(F32)).astype(BF16)
-                base = part * 2 * WIDE + block * 4
+                at = pl.ds(first_group * STEPS + late * count, count)
+                wait_bytes(partial_in.at[at], partial_recv.at[part * STEPS + late])
+                other = partial_in[at].reshape(rows, COLS).astype(F32)
+                total = (kept[late, :rows] + other).astype(BF16)
+                base = block * 4
                 for where in (0, 1):
                     for q in range(4):
-                        returning[base + where * WIDE + q] = total[
-                            where * PART : (where + 1) * PART, q * LANE : (q + 1) * LANE
-                        ]
+                        returning[base + where * WIDE + q, first_group : first_group + count] = total[
+                            where * size : (where + 1) * size, q * LANE : (q + 1) * LANE
+                        ].reshape(count, GROUP_SLOTS, LANE)
                 for q in range(4):
                     spot = flipped(me % 4, q, 2)
                     target = block * 4 + spot
                     for turn in (0, 1):
                         where = high if turn == 0 else 1 - high
-                        slot = returning.at[base + where * WIDE + spot]
-                        home = returned.at[part * 2 * WIDE + high * WIDE + me]
+                        slot = returning.at[base + where * WIDE + spot, groups]
+                        home = returned.at[high * WIDE + me, groups]
                         sems = back_send.at[part], back_recv.at[part, high]
                         if turn == 1 or q > 0:
                             remote(slot, home, *sems, target, where * 2 + core).start()
@@ -609,35 +676,34 @@
 
                             @pl.when(late == 0)
                             def _():
-                                pltpu.make_async_copy(slot, home, local_sem.at[10 + part]).start()
+                                pltpu.make_async_copy(slot, home, local_sem.at[11 + part]).start()
 
             return carry
 
         lax.fori_loop(0, STEPS + LAG, step, 0)
 
     def combine(part):
-        wait_bytes(returned.at[0], local_sem.at[10 + part])
-        wait_bytes(returned.at[pl.ds(0, WIDE - 1)], back_recv.at[part, high])
-        wait_bytes(returned.at[pl.ds(0, WIDE)], back_recv.at[part, 1 - high])
-        for g in (2 * part, 2 * part + 1):
-            at = (g % 2) * GROUP_SLOTS
+        first_group, count = PARTS[part]
+        groups = pl.ds(first_group, count)
+        wait_bytes(returned.at[0, groups], local_sem.at[11 + part])
+        wait_bytes(returned.at[pl.ds(0, WIDE - 1), groups], back_recv.at[part, high])
+        wait_bytes(returned.at[pl.ds(0, WIDE), groups], back_recv.at[part, 1 - high])
+        for g in range(first_group, first_group + count):
             picks = [jnp.zeros((LANE, LANE), F32)] * 2
             for where in (0, 1):
                 for s in (0, 1):
-                    rows = jnp.concatenate(
-                        [
-                            returned[(part * 2 + where) * WIDE + 2 * e + s, at : at + GROUP_SLOTS, :]
-                            for e in range(EXPERTS)
-                        ],
-                        axis=0,
-                    )
+                    rows = jnp.concatenate([returned[where * WIDE + 2 * e + s, g] for e in range(EXPERTS)], axis=0)
                     picks = [picks[k] + dot(placed[g, k], rows) for k in (0, 1)]
             weight = to_column(heavy[g : g + 1])
             result[g * LANE : (g + 1) * LANE] = (
                 residual[g * LANE : (g + 1) * LANE].astype(F32) + weight * picks[0] + (1.0 - weight) * picks[1]
             ).astype(BF16)
 
-    swaps = receive(0)
+    receive(0)
+    for load in loads:
+        load.wait()
+    experts(0)
+    experts(1)
 
     collect(stats, stats_in, 0)
     averages = jnp.zeros((GROUPS, LANE), F32)
@@ -664,20 +730,15 @@
         diffs[g : g + 1, :] = to_row(lead)
         diffs[GROUPS + g : GROUPS + g + 1, :] = jnp.zeros((1, LANE), F32)
     share(diffs, diffs_in, 1)
-
-    for load in loads:
-        load.wait()
-    experts(0)
-    swaps += receive(1)
-    experts(1)
+    experts(2)
 
     collect(diffs, diffs_in, 1)
     leads = jnp.zeros((GROUPS, LANE), F32)
     for w in range(WIDE):
         leads += diffs_in[w, :GROUPS]
     heavy = 1.0 / (1.0 + jnp.exp(-leads))
-    combine(0)
-    combine(1)
+    for part in range(len(PARTS)):
+        combine(part)
 
     spread.finish()
     spread2.finish()
@@ -686,21 +747,34 @@
     for which in range(2):
         wait_bytes(columns.at[0, pl.ds(0, WIDE - 1)], column_send.at[which])
         wait_bytes(stats_in.at[pl.ds(0, WIDE - 1)], small_send.at[which])
-        wait_bytes(arrived.at[pl.ds(0, 2 * WIDE - 1)], out_send.at[which])
-        wait_bytes(returned.at[pl.ds(0, 2 * WIDE - 1)], back_send.at[which])
     for half in (0, 1):
-        for other in range(NARROW):
-
-            @pl.when(other > n)
-            def _():
-                wait_bytes(fresh(parity, n, half), kv_send.at[0, half, other])
-
-            @pl.when(other >= n)
-            def _():
-                wait_bytes(fresh(parity, n, half), kv_send.at[1, half, other])
-
-    for at in range(2 * STEPS):
-        wait_bytes(partial_out.at[at], partial_send.at[at])
+
+        def sent(order, half=half):
+            wait_bytes(fresh(parity, n, half), kv_send.at[half, order])
+
+        sent(0)
+
+        @pl.when(high == 0)
+        def _():
+            sent(1)
+            sent(2)
+
+        @pl.when(core == 0)
+        def _():
+            sent(3)
+            sent(4)
+
+        @pl.when(high == 1)
+        def _():
+            sent(5)
+            sent(6)
+
+    for part, (first_group, count) in enumerate(PARTS):
+        groups = pl.ds(first_group, count)
+        wait_bytes(arrived.at[pl.ds(0, 2 * WIDE - 1), groups], out_send.at[part])
+        wait_bytes(returned.at[pl.ds(0, 2 * WIDE - 1), groups], back_send.at[part])
+        for k in range(STEPS):
+            wait_bytes(partial_out.at[pl.ds(0, count)], partial_send.at[part * STEPS + k])
 
 
 def body(
@@ -744,6 +818,9 @@
             held(ROWS, LANE),
             held(ROWS, LANE),
             held(ROWS, LANE),
+            held(ROWS, LANE, kind=F32),
+            held(2, ROWS, LANE, kind=F32),
+            held(ROWS, LANE, kind=F32),
             held(HIDDEN, D),
             held(HIDDEN, D),
             held(HIDDEN, D),
@@ -752,36 +829,36 @@
             held(2 * GROUPS, LANE, kind=F32),
             held(WIDE, 2 * GROUPS, LANE, kind=F32),
             held(GROUPS, 2, LANE, EXPERTS * GROUP_SLOTS),
-            held(2, EXPERTS, PART, LANE),
-            held(2 * ALL, PART, LANE),
+            held(EXPERTS, GROUPS, GROUP_SLOTS, LANE),
+            held(ALL, GROUPS, GROUP_SLOTS, LANE),
             held(2 * LANE, D),
             held(2 * LANE, HIDDEN),
-            held(2 * STEPS, LANE, COLS),
-            held(2 * STEPS, LANE, COLS),
+            held(GROUPS * STEPS, OWN, COLS),
+            held(GROUPS * STEPS, OWN, COLS),
             held(STEPS, LANE, COLS, kind=F32),
-            held(4 * WIDE, PART, LANE),
-            held(4 * WIDE, PART, LANE),
+            held(2 * WIDE, GROUPS, GROUP_SLOTS, LANE),
+            held(2 * WIDE, GROUPS, GROUP_SLOTS, LANE),
             dma((SENDS,)),
             dma((2, WIDE)),
             dma((SENDS,)),
             dma((2, WIDE)),
-            dma((12,)),
+            dma((11 + len(PARTS),)),
             dma((2,)),
             dma((2,)),
             dma((4,)),
-            dma((2, 2, NARROW)),
+            dma((2, 7)),
             dma((2, 2, NARROW)),
             dma((3,)),
             dma((2,)),
             dma((2,)),
-            dma((2,)),
-            dma((2, 2)),
-            dma((2, 2)),
-            dma((2, 2)),
-            dma((2 * STEPS,)),
-            dma((2 * STEPS,)),
-            dma((2,)),
-            dma((2, 2)),
+            dma((len(PARTS),)),
+            dma((len(PARTS), 2)),
+            dma((len(PARTS), 2)),
+            dma((len(PARTS), 2)),
+            dma((len(PARTS) * STEPS,)),
+            dma((len(PARTS) * STEPS,)),
+            dma((len(PARTS),)),
+            dma((len(PARTS), 2)),
         ],
         compiler_params=pltpu.CompilerParams(
             collective_id=0, has_side_effects=True, vmem_limit_bytes=60 * 2**20

time: 166 us -> 157 us (0.946)
  Pallas kernels: 164 us -> 155 us
    pallas_call x1, Pallas kernels: 164 us -> 155 us  [body(): pl.pallas_call(layer_kernel, out_shape=jax.ShapeDtypeStruct((ROWS, LANE),...]
where the time goes in v3:
time: 157 us
  Pallas kernels  155 us (99%)
  local copies, waits for them, and re-layouts  1.57 us (1%)
    pallas_call x1, Pallas kernels, body(): pl.pallas_call(layer_kernel, out_shape=jax.ShapeDtypeStruct((ROWS, LANE),...  155 us

profile of v3, /device:TPU:1, one launch (start us, length us, event | category | flops | bytes accessed | tf_op | source)
XLA Modules:
  0.0 157.0 jit_solution(16528944002654875976)
XLA Ops:
  0.0 155.4 %shard_map.136 = bf16[512,128]{1,0:T(8,128)(2,1)} custom-call(bf16[512,128]{1,0:T(8,128)(2,1)} %hidden.1, f32[32,128]{1,0:T(8,128)} %bitcast.9, bf16[4096,128]{1,0:T(8,128)(2,1)} %query_weight.1, bf16[128,1024]{1,0:T(8,128)(2,1)} %key_weight.1, bf16[128,1024]{1,0:T(8,128)(2,1)} %value_weight.1, bf16[128,4096]{1,0:T(8,128)(2,1)} %out_weight.1, ...), custom_call_target="tpu_custom_call" | custom-call | tf_op jit(solution)/shard_map/pallas_call | solution.py:803
  155.4 1.6 copy.16

commit v4 on v3

--- a/solution.py
+++ b/solution.py
@@ -180,7 +180,7 @@
 OWN = 2 * GROUP_SLOTS
 COLS = 512
 STEPS = D // COLS
-LAG = 2
+LAG = 4
 BITS = 5
 ALL = NARROW * WIDE
 

time: 157 us -> 156 us (level)
  no operation moved by 1% of the time
where the time goes in v4:
time: 156 us
  Pallas kernels  154 us (99%)
  local copies, waits for them, and re-layouts  1.57 us (1%)
    pallas_call x1, Pallas kernels, body(): pl.pallas_call(layer_kernel, out_shape=jax.ShapeDtypeStruct((ROWS, LANE),...  154 us

profile of v4, /device:TPU:1, one launch (start us, length us, event | category | flops | bytes accessed | tf_op | source)
XLA Modules:
  0.0 155.9 jit_solution(5118241972131090372)
XLA Ops:
  0.0 154.4 %shard_map.136 = bf16[512,128]{1,0:T(8,128)(2,1)} custom-call(bf16[512,128]{1,0:T(8,128)(2,1)} %hidden.1, f32[32,128]{1,0:T(8,128)} %bitcast.9, bf16[4096,128]{1,0:T(8,128)(2,1)} %query_weight.1, bf16[128,1024]{1,0:T(8,128)(2,1)} %key_weight.1, bf16[128,1024]{1,0:T(8,128)(2,1)} %value_weight.1, bf16[128,4096]{1,0:T(8,128)(2,1)} %out_weight.1, ...), custom_call_target="tpu_custom_call" | custom-call | tf_op jit(solution)/shard_map/pallas_call | solution.py:803
  154.4 1.6 %copy.16 = bf16[512,128]{1,0:T(8,128)(2,1)} copy(bf16[512,128]{1,0:T(8,128)(2,1)} %shard_map.136) | data formatting | bytes 262144

commit v5 on v4

--- a/solution.py
+++ b/solution.py
@@ -288,9 +288,8 @@
     greet(
         [
             (WIDE - 1, lambda i: ((me + 1 + i) % WIDE, n)),
-            (WIDE, lambda i: ((me + i) % WIDE, far)),
-            (2, lambda i: (me, partner + i * (across - partner))),
-            (2, lambda i: (mate, partner + i * (across - partner))),
+            (2, lambda i: (me, partner + i * (far - partner))),
+            (1, lambda i: (mate, far)),
         ]
     )
 

time: 156 us -> 156 us (level)
  no operation moved by 1% of the time
where the time goes in v5:
time: 156 us
  Pallas kernels  155 us (99%)
  local copies, waits for them, and re-layouts  1.57 us (1%)
    pallas_call x1, Pallas kernels, body(): pl.pallas_call(layer_kernel, out_shape=jax.ShapeDtypeStruct((ROWS, LANE),...  155 us

profile of v5, /device:TPU:1, one launch (start us, length us, event | category | flops | bytes accessed | tf_op | source)
XLA Modules:
  0.0 156.3 jit_solution(3104070917596735229)
XLA Ops:
  0.0 154.7 %shard_map.136 = bf16[512,128]{1,0:T(8,128)(2,1)} custom-call(bf16[512,128]{1,0:T(8,128)(2,1)} %hidden.1, f32[32,128]{1,0:T(8,128)} %bitcast.9, bf16[4096,128]{1,0:T(8,128)(2,1)} %query_weight.1, bf16[128,1024]{1,0:T(8,128)(2,1)} %key_weight.1, bf16[128,1024]{1,0:T(8,128)(2,1)} %value_weight.1, bf16[128,4096]{1,0:T(8,128)(2,1)} %out_weight.1, ...), custom_call_target="tpu_custom_call" | custom-call | tf_op jit(solution)/shard_map/pallas_call | solution.py:802
  154.7 1.6 %copy.16 = bf16[512,128]{1,0:T(8,128)(2,1)} copy(bf16[512,128]{1,0:T(8,128)(2,1)} %shard_map.136) | data formatting | bytes 262144
